TPU v7x, 256 devices: a whole 4x4x8 slice. The times are simulated.
256 devices in a mesh: batch: 8 (over y, core), expert: 32 (over z, x).
Axes of the slice: x: 4, y: 4, z: 8, core: 2. Of those that a mesh axis runs over, the one named last changes fastest.
Arguments:
- layer_in: bfloat16 [2, 32, 64, 2048], P(None, 'expert', 'batch'), may hold values from -6 to 6
- queries: bfloat16 [2, 32, 64, 2048], P(None, 'expert', 'batch'), may hold values from -6 to 6
- fresh_entries: bfloat16 [2, 32, 64, 4096], P(None, 'expert', 'batch'), may hold values from -6 to 6
- cross_queries: bfloat16 [2, 32, 64, 2048], P(None, 'expert', 'batch'), may hold values from -6 to 6
- past_cache: bfloat16 [32, 64, 14, 4096], P('expert', 'batch'), may hold values from -5 to 5
- encoder_states: bfloat16 [32, 16, 32, 4096], P('expert', 'batch'), may hold values from -5 to 5
- source_lengths: int32 [32, 16], P('expert', 'batch'), may hold values from 2 to 32, as said below
- parents: int32 [2, 32, 64], P(None, 'expert'), may hold values from 0 to 63, as said below
- expert_ids: int32 [2, 32, 64, 2], P(None, 'expert'), may hold values from 0 to 63, all different within a row; in each aligned block of 64 rows (0 to 63, 64 to 127, ..., all dimensions but the last counted through in order) at most 4 rows name the same one
- gate_weights: float32 [2, 32, 64, 2], P(None, 'expert'), may hold values from 0.2 to 1
- norm_gain: bfloat16 [2048], replicated, may hold values from 0.25 to 1.75
- up_weight: bfloat16 [64, 2048, 4096], P('expert', None, 'batch'), may hold values from -0.125 to 0.125
- down_weight: bfloat16 [64, 4096, 2048], P('expert', 'batch'), may hold values from -0.09375 to 0.09375
Outputs:
- layer_out: bfloat16 [2, 32, 64, 2048], P(None, 'expert', 'batch')
- cache_out: bfloat16 [32, 64, 16, 4096], P('expert', 'batch')
Inputs may be any that keep to these rules, and one draw needn't show every extreme that they name: For each step and group, parents is a permutation of the group's 64 rows, numbered within the group; rows with equal r // 8 are one device's slots. The slots of one device take exactly 2 rows held by other devices, at most one from each, and give exactly 2 of their rows to other devices, at most one to each. `expert_ids`: each row names two different experts. Within one step and one group no expert is named by more than 4 rows. `source_lengths`: in every group some sentence has all 32 positions.
All inputs are finite; a program needn't handle non-finite values.
Results may differ from a plain program's by a relative error of at most 0.0044.
Values may be sent and summed in bfloat16 or wider, within the bound.
A program may use at most 64 MiB of HBM per device.

v0:
```python
import jax
import jax.numpy as jnp
from jax import lax
from jax.sharding import PartitionSpec as P

HEADS = 16
DH = 128
CAP = 4
MOVE = 2
STEPS = 2


def normalize(residual_state, norm_gain):
    centered = residual_state - jnp.mean(residual_state, axis=-1, keepdims=True)
    variance = jnp.mean(centered * centered, axis=-1, keepdims=True)
    return (centered * lax.rsqrt(variance + 1e-05) * norm_gain.astype(jnp.float32)).astype(
        jnp.bfloat16
    )


def soft_weights(scores):
    highest = jnp.max(scores, axis=-1, keepdims=True)
    raised = jnp.exp(scores - highest)
    return (raised / jnp.sum(raised, axis=-1, keepdims=True)).astype(jnp.bfloat16)


def self_attend(queries_now, keys_all):
    row_count, key_count = (keys_all.shape[0], keys_all.shape[1])
    model_width = queries_now.shape[1]
    key_part = keys_all[:, :, :model_width].reshape(row_count, key_count, HEADS, DH)
    value_part = keys_all[:, :, model_width:].reshape(row_count, key_count, HEADS, DH)
    scores = jnp.einsum(
        "rhd,rphd->rhp",
        queries_now.reshape(row_count, HEADS, DH),
        key_part,
        preferred_element_type=jnp.float32,
    ) / jnp.sqrt(jnp.float32(DH))
    weights = soft_weights(scores)
    return jnp.einsum(
        "rhp,rphd->rhd", weights, value_part, preferred_element_type=jnp.float32
    ).reshape(row_count, model_width)


def cross_attend(queries_now, encoded, lengths):
    sentences, key_count = (encoded.shape[0], encoded.shape[1])
    row_count, model_width = queries_now.shape
    beam_size = row_count // sentences
    key_part = encoded[:, :, :model_width].reshape(sentences, key_count, HEADS, DH)
    value_part = encoded[:, :, model_width:].reshape(sentences, key_count, HEADS, DH)
    query_part = queries_now.reshape(sentences, beam_size, HEADS, DH)
    scores = jnp.einsum(
        "sbhd,sphd->sbhp", query_part, key_part, preferred_element_type=jnp.float32
    ) / jnp.sqrt(jnp.float32(DH))
    valid_mask = jnp.arange(key_count)[None, :] < lengths[:, None]
    scores = jnp.where(valid_mask[:, None, None, :], scores, -jnp.inf)
    weights = soft_weights(scores)
    return jnp.einsum(
        "sbhp,sphd->sbhd", weights, value_part, preferred_element_type=jnp.float32
    ).reshape(row_count, model_width)


def reorder(cache_rows, order_rows, position, devices, slots):
    group_rows = order_rows.shape[0]
    source_dev = order_rows // slots
    source_row = order_rows % slots
    target_dev = jnp.arange(group_rows, dtype=jnp.int32) // slots
    own_dev = lax.dynamic_slice_in_dim(source_dev, position * slots, slots)
    own_row = lax.dynamic_slice_in_dim(source_row, position * slots, slots)
    crossing = source_dev != target_dev
    matches = (order_rows[None, :] == jnp.arange(group_rows, dtype=jnp.int32)[:, None]) & crossing[
        None, :
    ]
    leaving = jnp.any(matches, axis=1).astype(jnp.int32).reshape(devices, slots)
    rank_table = jnp.cumsum(leaving, axis=1) - leaving
    own_leaving = lax.dynamic_index_in_dim(leaving, position, 0, keepdims=False)
    own_ranks = lax.dynamic_index_in_dim(rank_table, position, 0, keepdims=False)
    wanted = (own_leaving[None, :] == 1) & (
        own_ranks[None, :] == jnp.arange(MOVE, dtype=jnp.int32)[:, None]
    )
    picked = jnp.sum(jnp.where(wanted, jnp.arange(slots, dtype=jnp.int32)[None, :], 0), axis=1)
    arrived = lax.all_gather(cache_rows[picked], "batch", axis=0, tiled=True)
    source_rank = lax.dynamic_slice_in_dim(
        rank_table.reshape(group_rows)[order_rows], position * slots, slots
    )
    fetch_index = jnp.where(own_dev == position, own_row, slots + own_dev * MOVE + source_rank)
    combined = jnp.concatenate([cache_rows, arrived], axis=0)
    return combined[fetch_index]


def expert_mix(normed, expert_ids, gate_weights, up_weight, down_weight):
    sections = normed.shape[0]
    gathered = lax.all_gather(normed, "batch", axis=1, tiled=True)
    group_rows, model_width = (gathered.shape[1], gathered.shape[2])
    owners = lax.axis_size("expert")
    local_experts = up_weight.shape[0]
    experts = owners * local_experts
    room_size = sections * CAP
    flat_ids = expert_ids.reshape(sections, group_rows * 2)
    onehot = (flat_ids[:, :, None] == jnp.arange(experts, dtype=jnp.int32)[None, None, :]).astype(
        jnp.int32
    )
    earlier = jnp.cumsum(onehot, axis=1) - onehot
    rank_now = jnp.sum(earlier * onehot, axis=2)
    section_ids = jnp.arange(sections, dtype=jnp.int32)[:, None]
    slot_ids = (flat_ids * room_size + section_ids * CAP + rank_now).reshape(
        sections * group_rows, 2
    )
    slot_range = jnp.arange(experts * room_size, dtype=jnp.int32)[:, None]
    layout = ((slot_ids[None, :, 0] == slot_range) | (slot_ids[None, :, 1] == slot_range)).astype(
        jnp.bfloat16
    )
    packed = jnp.dot(
        layout,
        gathered.reshape(sections * group_rows, model_width),
        preferred_element_type=jnp.float32,
    ).astype(jnp.bfloat16)
    packed = packed.reshape(owners, local_experts, room_size, model_width)
    inner_act = jnp.einsum(
        "nxcd,xdh->nxch",
        lax.all_to_all(packed, "expert", split_axis=0, concat_axis=0, tiled=True),
        up_weight,
        preferred_element_type=jnp.float32,
    )
    inner_act = jax.nn.relu(inner_act).astype(jnp.bfloat16)
    expert_out = jnp.einsum(
        "nxch,xhd->nxcd", inner_act, down_weight, preferred_element_type=jnp.float32
    )
    returned = lax.all_to_all(
        expert_out, "expert", split_axis=0, concat_axis=0, tiled=True
    ).reshape(experts * room_size, model_width)
    picked = returned[slot_ids]
    weighted = jnp.sum(picked * gate_weights.reshape(sections * group_rows, 2)[:, :, None], axis=1)
    return lax.psum_scatter(
        weighted.reshape(sections, group_rows, model_width),
        "batch",
        scatter_dimension=1,
        tiled=True,
    )


def shards(
    layer_in,
    queries,
    fresh_entries,
    cross_queries,
    past_cache,
    encoder_states,
    source_lengths,
    parents,
    expert_ids,
    gate_weights,
    norm_gain,
    up_weight,
    down_weight,
):
    slots = past_cache.shape[1]
    devices = lax.axis_size("batch")
    position = lax.axis_index("batch")
    cache_now = past_cache[0]
    states = []
    mix_list = []
    for step_index in range(STEPS):
        cache_now = reorder(cache_now, parents[step_index, 0], position, devices, slots)
        extended = jnp.concatenate([cache_now, fresh_entries[step_index, 0][:, None, :]], axis=1)
        attended = self_attend(queries[step_index, 0], extended)
        crossed = cross_attend(cross_queries[step_index, 0], encoder_states[0], source_lengths[0])
        residual_state = layer_in[step_index, 0].astype(jnp.float32) + attended + crossed
        normed = normalize(residual_state, norm_gain)
        states.append(residual_state)
        mix_list.append(
            expert_mix(
                normed[None],
                expert_ids[step_index : step_index + 1, 0],
                gate_weights[step_index : step_index + 1, 0],
                up_weight,
                down_weight,
            )[0]
        )
        cache_now = extended
    total_mix = jnp.stack(mix_list)
    layer_out = (jnp.stack(states) + total_mix).astype(jnp.bfloat16)[:, None]
    return (layer_out, cache_now[None])


def solution(mesh):
    in_specs = (
        P(None, "expert", "batch", None),
        P(None, "expert", "batch", None),
        P(None, "expert", "batch", None),
        P(None, "expert", "batch", None),
        P("expert", "batch", None, None),
        P("expert", "batch", None, None),
        P("expert", "batch"),
        P(None, "expert", None),
        P(None, "expert", None, None),
        P(None, "expert", None, None),
        P(),
        P("expert", None, "batch"),
        P("expert", "batch", None),
    )
    out_specs = (P(None, "expert", "batch", None), P("expert", "batch", None, None))
    return jax.shard_map(shards, mesh=mesh, in_specs=in_specs, out_specs=out_specs, check_vma=False)
```

profile of v0, /device:TPU:1, one launch (start us, length us, event | category | flops | bytes accessed | tf_op | source)
XLA Modules:
  0.0 329.7 jit_solution(9624295397580459672)
XLA Ops:
  20.0 25.0 %all-gather.5.cloned.1.call-done = bf16[16,14,4096]{2,1,0:T(8,128)(2,1)} async-done(((bf16[2,14,4096]{2,1,0:T(8,128)(2,1)}), bf16[16,14,4096]{2,1,0:T(8,128)(2,1)}) %all-gather.5.cloned.1.call-update) | async-done | bytes 1835024 | tf_op jit(solution)/shard_map/all_gather | solution.py:81
  45.0 3.6 %pad_maximum_fusion = bf16[24,14,4096]{2,1,0:T(8,128)(2,1)} fusion(bf16[16,14,4096]{2,1,0:T(8,128)(2,1)} %all-gather.5.cloned.1.call-done, bf16[8,14,4096]{2,1,0:T(8,128)(2,1)S(1)} %bitcast.275), kind=kLoop, calls=%fused_computation.20 | loop fusion | flops 1376256 | bytes 5505024 | tf_op jit(solution)/shard_map/concatenate | solution.py:86
  48.6 2.5 gather_fusion.2
  59.5 21.4 %all-gather.7.cloned.1.call-done = bf16[16,15,4096]{2,1,0:T(8,128)(2,1)} async-done(((bf16[2,15,4096]{2,1,0:T(8,128)(2,1)}), bf16[16,15,4096]{2,1,0:T(8,128)(2,1)}) %all-gather.7.cloned.1.call-update) | async-done | bytes 1966096 | tf_op jit(solution)/shard_map/all_gather | solution.py:81
  81.0 3.9 %pad_maximum_fusion.1 = bf16[24,15,4096]{2,1,0:T(8,128)(2,1)} fusion(bf16[16,15,4096]{2,1,0:T(8,128)(2,1)} %all-gather.7.cloned.1.call-done, bf16[8,1,4096]{2,1,0:T(2,128)(2,1)S(1)} %copy.120, bf16[8,14,4096]{2,1,0:T(8,128)(2,1)S(1)} %gather_fusion.2), kind=kLoop, calls=%fused_computation.21 | loop fusion | flops 8847360 | bytes 5898240 | tf_op jit(solution)/shard_map/concatenate | solution.py:86
  84.9 2.5 gather_fusion.5
  90.5 12.9 %all_gather.14 = bf16[1,64,2048]{2,1,0:T(8,128)(2,1)S(1)} all-gather(bf16[1,8,2048]{2,1,0:T(8,128)(2,1)S(1)} %get-tuple-element.18), channel_id=1, replica_groups=mesh['batch'=8,'expert'=32] {'batch'}, dimensions={1}, use_global_device_ids=true | all-gather | bytes 294912 | tf_op jit(solution)/shard_map/all_gather | solution.py:92
  105.0 9.5 %all-to-all-start = ((bf16[32,2,4,2048]{3,2,1,0:T(4,128)(2,1)}), bf16[32,2,4,2048]{3,2,1,0:T(4,128)(2,1)S(1)}, u32[]{:S(2)}, u32[]{:S(2)}) async-start(bf16[32,2,4,2048]{3,2,1,0:T(4,128)(2,1)} %reshape.909), calls=%async_computation | async-start | bytes 2097152 | tf_op jit(solution)/shard_map/all_to_all | solution.py:120
  114.6 13.3 %all_gather.15 = bf16[1,64,2048]{2,1,0:T(8,128)(2,1)S(1)} all-gather(bf16[1,8,2048]{2,1,0:T(8,128)(2,1)} %get-tuple-element.19), channel_id=1, replica_groups=mesh['batch'=8,'expert'=32] {'batch'}, dimensions={1}, use_global_device_ids=true | all-gather | bytes 294912 | tf_op jit(solution)/shard_map/all_gather | solution.py:92
  129.6 12.1 %all-to-all-done = bf16[32,2,4,2048]{3,2,1,0:T(4,128)(2,1)S(1)} async-done(((bf16[32,2,4,2048]{3,2,1,0:T(4,128)(2,1)}), bf16[32,2,4,2048]{3,2,1,0:T(4,128)(2,1)S(1)}, u32[]{:S(2)}, u32[]{:S(2)}) %all-to-all-start) | async-done | bytes 1048608 | tf_op jit(solution)/shard_map/all_to_all | solution.py:120
  142.7 6.2 %all-to-all-start.2 = ((bf16[32,2,4,2048]{3,2,1,0:T(4,128)(2,1)}), bf16[32,2,4,2048]{3,2,1,0:T(4,128)(2,1)}, u32[]{:S(2)}, u32[]{:S(2)}) async-start(bf16[32,2,4,2048]{3,2,1,0:T(4,128)(2,1)} %reshape.916), calls=%async_computation.3 | async-start | bytes 2097152 | tf_op jit(solution)/shard_map/all_to_all | solution.py:120
  148.9 5.6 %fusion.12 = f32[32,2,4,2048]{3,0,2,1:T(8,128)S(1)} fusion(bf16[2,512,2048]{2,1,0:T(8,128)(2,1)} %param.25, bf16[2,2048,512]{2,1,0:T(8,128)(2,1)} %param.24, bf16[32,2,4,2048]{3,2,1,0:T(4,128)(2,1)} %copy-done.1), kind=kOutput, calls=%fused_computation.22 | convolution fusion | flops 1074003968 | bytes 11534336 | tf_op jit(solution)/shard_map/nxch,xhd->nxcd/dot_general | solution.py:125
  154.5 2.6 copy.138
  157.1 17.2 %all-to-all-done.2 = bf16[32,2,4,2048]{3,2,1,0:T(4,128)(2,1)} async-done(((bf16[32,2,4,2048]{3,2,1,0:T(4,128)(2,1)}), bf16[32,2,4,2048]{3,2,1,0:T(4,128)(2,1)}, u32[]{:S(2)}, u32[]{:S(2)}) %all-to-all-start.2) | async-done | bytes 1048608 | tf_op jit(solution)/shard_map/all_to_all | solution.py:120
  174.3 6.7 %all-to-all-start.1 = ((f32[32,2,4,2048]{3,2,1,0:T(4,128)}), f32[32,2,4,2048]{3,2,1,0:T(4,128)S(1)}, u32[]{:S(2)}, u32[]{:S(2)}) async-start(f32[32,2,4,2048]{3,2,1,0:T(4,128)} %copy.138), calls=%async_computation.1 | async-start | bytes 4194304 | tf_op jit(solution)/shard_map/all_to_all | solution.py:128
  181.0 6.9 %fusion.15 = f32[32,2,4,2048]{3,0,2,1:T(8,128)} fusion(bf16[2,512,2048]{2,1,0:T(8,128)(2,1)} %param.25, bf16[2,2048,512]{2,1,0:T(8,128)(2,1)} %param.24, bf16[32,2,4,2048]{3,2,1,0:T(4,128)(2,1)} %all-to-all-done.2), kind=kOutput, calls=%fused_computation.23 | convolution fusion | flops 1074003968 | bytes 11534336 | tf_op jit(solution)/shard_map/nxch,xhd->nxcd/dot_general | solution.py:125
  187.9 4.3 %copy.148 = f32[32,2,4,2048]{3,2,1,0:T(4,128)} copy(f32[32,2,4,2048]{3,0,2,1:T(8,128)} %fusion.15) | data formatting | bytes 4194304 | tf_op jit(solution)/shard_map/nxch,xhd->nxcd/transpose | solution.py:125
  192.2 35.4 %all-to-all-done.1 = f32[32,2,4,2048]{3,2,1,0:T(4,128)S(1)} async-done(((f32[32,2,4,2048]{3,2,1,0:T(4,128)}), f32[32,2,4,2048]{3,2,1,0:T(4,128)S(1)}, u32[]{:S(2)}, u32[]{:S(2)}) %all-to-all-start.1) | async-done | bytes 2097184 | tf_op jit(solution)/shard_map/all_to_all | solution.py:128
  227.6 7.3 %all-to-all-start.3 = ((f32[32,2,4,2048]{3,2,1,0:T(4,128)}), f32[32,2,4,2048]{3,2,1,0:T(4,128)}, u32[]{:S(2)}, u32[]{:S(2)}) async-start(f32[32,2,4,2048]{3,2,1,0:T(4,128)} %copy.148), calls=%async_computation.4 | async-start | bytes 4194304 | tf_op jit(solution)/shard_map/all_to_all | solution.py:128
  242.2 2.0 reshape.910
  248.0 3.1 multiply_reduce_fusion.1
  252.3 28.8 %all-to-all-done.3 = f32[32,2,4,2048]{3,2,1,0:T(4,128)} async-done(((f32[32,2,4,2048]{3,2,1,0:T(4,128)}), f32[32,2,4,2048]{3,2,1,0:T(4,128)}, u32[]{:S(2)}, u32[]{:S(2)}) %all-to-all-start.3) | async-done | bytes 2097184 | tf_op jit(solution)/shard_map/all_to_all | solution.py:128
  287.0 3.1 multiply_reduce_fusion
  291.4 30.2 %reduce-scatter.5.cloned.1.call-done = f32[1,8,2048]{2,1,0:T(8,128)} async-done(((f32[1,64,2048]{2,1,0:T(8,128)}), f32[1,8,2048]{2,1,0:T(8,128)}) %reduce-scatter.5.cloned.1.call-update) | async-done | bytes 65552 | tf_op jit(solution)/shard_map/reduce_scatter | solution.py:133
  (197 shorter events, 48.9 us)
Async XLA Ops:
  7.2 10.1 %copy-start.12 = (s32[2,1,64]{2,1,0:T(1,128)S(1)}, s32[2,1,64]{2,1,0:T(1,128)}, u32[]{:S(2)}) copy-start(s32[2,1,64]{2,1,0:T(1,128)} %param.20) | copy-start | bytes 1540
  7.2 7.5 %copy-start.9 = (bf16[2,1,8,2048]{3,2,1,0:T(8,128)(2,1)S(1)}, bf16[2,1,8,2048]{3,2,1,0:T(8,128)(2,1)}, u32[]{:S(2)}) copy-start(bf16[2,1,8,2048]{3,2,1,0:T(8,128)(2,1)} %param.16) | copy-start | bytes 196612
  7.2 8.2 %copy-start.17 = (bf16[2048]{0:T(1024)(128)(2,1)S(1)}, bf16[2048]{0:T(1024)(128)(2,1)}, u32[]{:S(2)}) copy-start(bf16[2048]{0:T(1024)(128)(2,1)} %param.23) | copy-start | bytes 12292
  7.2 8.2 %copy-start.11 = (s32[2,1,64,2]{2,3,1,0:T(2,128)S(1)}, s32[2,1,64,2]{2,3,1,0:T(2,128)}, u32[]{:S(2)}) copy-start(s32[2,1,64,2]{2,3,1,0:T(2,128)} %param.21) | copy-start | bytes 3076
  7.2 12.0 %copy-start.21 = (s32[1,2]{1,0:T(1,128)S(1)}, s32[1,2]{1,0:T(1,128)}, u32[]{:S(2)}) copy-start(s32[1,2]{1,0:T(1,128)} %param.19) | copy-start | bytes 28
  7.2 12.0 %copy-start.5 = (bf16[1,2,32,4096]{3,2,1,0:T(8,128)(2,1)S(1)}, bf16[1,2,32,4096]{3,2,1,0:T(8,128)(2,1)}, u32[]{:S(2)}) copy-start(bf16[1,2,32,4096]{3,2,1,0:T(8,128)(2,1)} %param.18) | copy-start | bytes 1572868
  7.2 37.8 %all-gather.5.cloned.1.call-start = ((), (), s32[]{:S(2)}) async-start(), calls=%async_computation.8 | async-start | bytes 2359296 | tf_op jit(solution)/shard_map/all_gather | solution.py:81
  12.9 68.1 %all-gather.7.cloned.1.call-start = ((), (), s32[]{:S(2)}) async-start(), calls=%async_computation.9 | async-start | bytes 2359296 | tf_op jit(solution)/shard_map/all_gather | solution.py:81
  20.0 37.6 %copy-start.6 = (bf16[2,4,16,8,128]{4,3,2,1,0:T(8,128)(2,1)}, bf16[2,4,16,8,128]{4,3,2,1,0:T(8,128)(2,1)S(1)}, u32[]{:S(2)}) copy-start(bf16[2,4,16,8,128]{4,3,2,1,0:T(8,128)(2,1)S(1)} %get-tuple-element.15) | copy-start | bytes 786436
  48.6 6.8 %copy-start.10 = (bf16[2,1,8,2048]{3,2,1,0:T(8,128)(2,1)S(1)}, bf16[2,1,8,2048]{3,2,1,0:T(8,128)(2,1)}, u32[]{:S(2)}) copy-start(bf16[2,1,8,2048]{3,2,1,0:T(8,128)(2,1)} %param.14) | copy-start | bytes 196612
  87.5 15.9 %copy-start.19 = (s32[64]{0:T(128)S(1)}, s32[64]{0:T(128)}, u32[]{:S(2)}) copy-start(s32[64]{0:T(128)} %get-tuple-element.36) | copy-start | bytes 772
  87.5 15.9 %copy-start.20 = (s32[64]{0:T(128)S(1)}, s32[64]{0:T(128)}, u32[]{:S(2)}) copy-start(s32[64]{0:T(128)} %get-tuple-element.37) | copy-start | bytes 772
  89.3 14.0 %copy-start.3 = (f32[2,4,16,128]{3,2,1,0:T(8,128)}, f32[2,4,16,128]{3,2,1,0:T(8,128)S(1)}, u32[]{:S(2)}) copy-start(f32[2,4,16,128]{3,2,1,0:T(8,128)S(1)} %copy.131) | copy-start | bytes 196612
  89.7 24.9 %copy-start.18 = (s32[64,2]{0,1:T(2,128)S(1)}, s32[64,2]{0,1:T(2,128)}, u32[]{:S(2)}) copy-start(s32[64,2]{0,1:T(2,128)} %get-tuple-element.33) | copy-start | bytes 1540
  105.0 36.6 %all-to-all-start = ((bf16[32,2,4,2048]{3,2,1,0:T(4,128)(2,1)}), bf16[32,2,4,2048]{3,2,1,0:T(4,128)(2,1)S(1)}, u32[]{:S(2)}, u32[]{:S(2)}) async-start(bf16[32,2,4,2048]{3,2,1,0:T(4,128)(2,1)} %reshape.909), calls=%async_computation | async-start | bytes 2097152 | tf_op jit(solution)/shard_map/all_to_all | solution.py:120
  142.7 31.6 %all-to-all-start.2 = ((bf16[32,2,4,2048]{3,2,1,0:T(4,128)(2,1)}), bf16[32,2,4,2048]{3,2,1,0:T(4,128)(2,1)}, u32[]{:S(2)}, u32[]{:S(2)}) async-start(bf16[32,2,4,2048]{3,2,1,0:T(4,128)(2,1)} %reshape.916), calls=%async_computation.3 | async-start | bytes 2097152 | tf_op jit(solution)/shard_map/all_to_all | solution.py:120
  174.3 53.3 %all-to-all-start.1 = ((f32[32,2,4,2048]{3,2,1,0:T(4,128)}), f32[32,2,4,2048]{3,2,1,0:T(4,128)S(1)}, u32[]{:S(2)}, u32[]{:S(2)}) async-start(f32[32,2,4,2048]{3,2,1,0:T(4,128)} %copy.138), calls=%async_computation.1 | async-start | bytes 4194304 | tf_op jit(solution)/shard_map/all_to_all | solution.py:128
  192.2 42.7 %copy-start.14 = (s32[128]{0:T(128)S(1)}, s32[128]{0:T(128)}, u32[]{:S(2)}) copy-start(s32[128]{0:T(128)} %copy-done.13) | copy-start | bytes 1540
  192.2 43.5 %copy-start.16 = (s32[128]{0:T(128)S(1)}, s32[128]{0:T(128)}, u32[]{:S(2)}) copy-start(s32[128]{0:T(128)} %copy-done.15) | copy-start | bytes 1540
  227.6 14.6 %copy-start = (f32[32,2,4,2048]{3,2,1,0:T(4,128)}, f32[32,2,4,2048]{3,2,1,0:T(4,128)S(1)}, u32[]{:S(2)}) copy-start(f32[32,2,4,2048]{3,2,1,0:T(4,128)S(1)} %all-to-all-done.1) | copy-start | bytes 6291460
  227.6 53.6 %all-to-all-start.3 = ((f32[32,2,4,2048]{3,2,1,0:T(4,128)}), f32[32,2,4,2048]{3,2,1,0:T(4,128)}, u32[]{:S(2)}, u32[]{:S(2)}) async-start(f32[32,2,4,2048]{3,2,1,0:T(4,128)} %copy.148), calls=%async_computation.4 | async-start | bytes 4194304 | tf_op jit(solution)/shard_map/all_to_all | solution.py:128
  234.9 56.6 %reduce-scatter.3.cloned.1.call-start = ((), (), s32[]{:S(2)}) async-start(), calls=%async_computation.6 | async-start | bytes 589824 | tf_op jit(solution)/shard_map/reduce_scatter | solution.py:133
  251.1 70.5 %reduce-scatter.5.cloned.1.call-start = ((), (), s32[]{:S(2)}) async-start(), calls=%async_computation.7 | async-start | bytes 589824 | tf_op jit(solution)/shard_map/reduce_scatter | solution.py:133
  285.1 5.1 %copy-start.4 = (f32[2,4,16,128]{3,2,1,0:T(8,128)S(1)}, f32[2,4,16,128]{3,2,1,0:T(8,128)}, u32[]{:S(2)}) copy-start(f32[2,4,16,128]{3,2,1,0:T(8,128)} %copy-done.3) | copy-start | bytes 196612
  (10 other events, 28.1 us)
Sparse Core Ops, SparseCore 0:
  13.0 31.9 all-gather.4
  52.9 28.0 all-gather.6
  251.2 34.5 reduce-scatter.2
  290.2 31.4 reduce-scatter.4
where the time goes:
time: 333 us; the launch traced here: 330 us
  waiting for transfers between devices  170 us (51%)
  local copies, waits for them, and re-layouts  46.6 us (14%)
  starting transfers between devices  30.1 us (9%)
  blocking collectives  26.2 us (8%)
  other arithmetic  24.9 us (7%)
  matrix products  17.2 us (5%)
  between operations  14.5 us (4%)
    all_to_all x2, waiting for transfers between devices, expert_mix(): lax.all_to_all(expert_out, 'expert', split_axis=0, concat_axis=0, tiled=T...  64.3 us
    all_gather x2, waiting for transfers between devices, reorder(): arrived = lax.all_gather(cache_rows[picked], 'batch', axis=0, tiled=True)  46.4 us
    reduce_scatter x2, waiting for transfers between devices, expert_mix(): lax.psum_scatter(weighted.reshape(sections, group_rows, model_width), 'ba...  30.2 us
    all_to_all x2, waiting for transfers between devices, expert_mix(): lax.all_to_all(packed, 'expert', split_axis=0, concat_axis=0, tiled=True)  29.3 us
    all_gather x2, blocking collectives, expert_mix(): gathered = lax.all_gather(normed, 'batch', axis=1, tiled=True)  26.2 us
    all_to_all x2, starting transfers between devices, expert_mix(): lax.all_to_all(packed, 'expert', split_axis=0, concat_axis=0, tiled=True)  15.7 us
    all_to_all x2, starting transfers between devices, expert_mix(): lax.all_to_all(expert_out, 'expert', split_axis=0, concat_axis=0, tiled=T...  13.9 us
    dot_general x2, matrix products, expert_mix(): jnp.einsum('nxch,xhd->nxcd', inner_act, down_weight, preferred_element_ty...  12.5 us
  transfers between devices with their start and end apart: 8, of which 7 were waited for; matrix products, arithmetic and copies ran while one was open for 19% of the time, Pallas kernels for 0%

commit v1 on v0

v1 whole, which is shorter than its diff:
```python
import functools

import jax
import jax.numpy as jnp
from jax import lax
from jax.experimental import pallas as pl
from jax.experimental.pallas import tpu as pltpu
from jax.sharding import PartitionSpec as P

HEADS = 16
DH = 128
CAP = 4
STEPS = 2
SLOTS = 8
BEAM = 4
NB = 8
ROWS = NB * SLOTS
PER = 2 * CAP
POS = 16
MESH = pl.DeviceIdType.MESH
F32 = jnp.float32
BF16 = jnp.bfloat16


def iota(shape, dim):
    return lax.broadcasted_iota(jnp.int32, shape, dim)


def plan_kernel(par_ref, out_ref):
    n = ROWS
    row_i, col_i = iota((n, n), 1), iota((n, n), 0)
    rowf, colf = row_i.astype(F32), col_i.astype(F32)
    dev_r, dev_c = jnp.floor(rowf * 0.125), jnp.floor(colf * 0.125)
    eye = (row_i == col_i).astype(F32)
    tri = jnp.where((row_i < col_i) & (dev_r == dev_c), 1.0, 0.0)

    def across(x):
        return jnp.broadcast_to(jnp.sum(x, axis=1, keepdims=True), (n, n))

    def down(x):
        return jnp.broadcast_to(jnp.sum(x, axis=0, keepdims=True), (n, n))

    def to_col(r):
        return across(eye * r)

    def to_row(c):
        return down(eye * c)

    def step(par):
        pr = jnp.broadcast_to(par.astype(F32), (n, n))
        pc = to_col(pr)
        hot = jnp.where(colf == pr, 1.0, 0.0)
        cross_r = jnp.where(jnp.floor(pr * 0.125) != dev_r, 1.0, 0.0)
        cross_c = to_col(cross_r)
        leave_c = across(hot * cross_r)
        leave_r = to_row(leave_c)
        pool_c = dev_c * 2 + across(tri * leave_r)
        src_c = to_col(down(hot * pool_c))
        arank_c = across(tri * cross_r)
        place = jnp.where(rowf == dev_c * 2 + arank_c, cross_c, 0.0)
        leave = jnp.where(rowf == pool_c, leave_c, 0.0)
        local_r = pr - 8 * jnp.floor(pr * 0.125)
        ext = jnp.where(cross_r > 0, 8 + to_row(arank_c), local_r)
        return pc, hot, cross_c, pool_c, src_c, place, leave, ext

    p0c, hot0, cross0, pool0, src0, place0, leave0, ext0 = step(par_ref[0:1, :])
    p1c, hot1, cross1, pool1, src1, place1, leave1, ext1 = step(par_ref[1:2, :])
    slot_c = colf - 8 * dev_c
    from_c = jnp.where(cross0 > 0, src0, 16 + pool1)
    kept_c = jnp.where(cross0 > 0, 0.0, p0c - 8 * jnp.floor(p0c * 0.125))
    srcc1 = to_col(down(hot1 * from_c))
    tables = (
        ext0,
        ext1,
        down(leave0 * slot_c),
        down(leave1 * kept_c),
        down(leave1 * slot_c),
        down(place0 * src0),
        down(place1 * srcc1),
        down(place1 * src1),
    )
    for k, table in enumerate(tables):
        out_ref[k : k + 1, :] = table[0:1, :].astype(jnp.int32)


def head_mask(rows):
    head = iota((rows, HEADS, HEADS * DH), 1)
    column = iota((rows, HEADS, HEADS * DH), 2) // DH
    return (head == column).astype(F32)


def attend(q, keys, values, valid):
    d = HEADS * DH
    mask = head_mask(SLOTS)
    spread = (jnp.broadcast_to(q[:, None, :], (SLOTS, HEADS, d)) * mask).reshape(SLOTS * HEADS, d)
    scores = lax.dot_general(
        spread.astype(BF16), keys, (((1,), (1,)), ((), ())), preferred_element_type=F32
    ) * (1.0 / DH**0.5)
    scores = jnp.where(valid, scores, -1e30)
    raised = jnp.where(valid, jnp.exp(scores - jnp.max(scores, axis=1, keepdims=True)), 0.0)
    weights = (raised / jnp.sum(raised, axis=1, keepdims=True)).astype(BF16)
    out = jnp.dot(weights, values, preferred_element_type=F32)
    return jnp.sum(out.reshape(SLOTS, HEADS, d) * mask, axis=1)


def layer_kernel(
    ne,
    tbl, lens, layer_in, queries, fresh, cross_q, cache, enc, ids, gates, gain, up_hbm, down_hbm,
    layer_out, cache_out,
    wup, wdn, freshf, st_a, pool0, pool1, st_b, cvx, ebuf, ext1, cross_s, resid,
    pack_p, gate_hi, gate_lo, hsend, hrecv, psend, xb, hid, sib_s, sib_r, ysend, yrecv,
    rsend, rrecv, fsend, frecv, wsem, lsem, csem, bsend, brecv, agsend, agrecv, sibsend, sibrecv,
):
    b, e = lax.axis_index("batch"), lax.axis_index("expert")
    y, c = b // 2, b % 2
    sib = y * 2 + (1 - c)
    d = HEADS * DH
    kc = 2 * d // NB
    mc = d // NB
    slots = ne * PER

    def peer_y(q):
        return lax.rem(y + q, 4)

    barrier = pltpu.get_barrier_semaphore()

    def greet_b(k, _):
        pl.semaphore_signal(
            barrier, inc=1, device_id=(lax.rem(b + k, NB), e), device_id_type=MESH
        )
        return 0

    def greet_e(k, _):
        pl.semaphore_signal(
            barrier, inc=1, device_id=(b, lax.rem(e + k, ne)), device_id_type=MESH
        )
        return 0

    lax.fori_loop(1, NB, greet_b, 0)
    lax.fori_loop(1, ne, greet_e, 0)

    up_copy = pltpu.make_async_copy(up_hbm, wup, wsem.at[0])
    down_copy = pltpu.make_async_copy(down_hbm, wdn, wsem.at[1])
    up_copy.start()
    down_copy.start()

    def local(src, dst):
        copy = pltpu.make_async_copy(src, dst, lsem)
        copy.start()
        copy.wait()

    def wait_bytes(ref, sem):
        pltpu.make_async_copy(ref, ref, sem).wait()

    position = iota((POS, 2 * d), 0)

    def to16(rows14):
        pad = jnp.zeros((POS - rows14.shape[0], rows14.shape[1]), F32)
        return jnp.concatenate([rows14.astype(F32), pad], axis=0)

    for t in range(STEPS):
        for r in range(SLOTS):
            freshf[t, r] = fresh[t, r : r + 1, :].astype(F32)
    for j in range(2):
        st_a[0, j] = to16(cache[tbl[2, b * 2 + j]]).astype(BF16)
        entry = jnp.broadcast_to(freshf[0, tbl[4, b * 2 + j]], (POS, 2 * d))
        st_a[1, j] = jnp.where(
            position == 14, entry, to16(cache[tbl[3, b * 2 + j]])
        ).astype(BF16)

    pl.semaphore_wait(barrier, NB - 1 + ne - 1)

    pools = (pool0, pool1)
    landing = (cvx, ebuf)

    def send_a(t):
        def one(k, _):
            to = lax.rem(b + k, NB)
            pltpu.make_async_remote_copy(
                st_a.at[t, :, :, pl.ds(pl.multiple_of(to * kc, kc), kc)],
                pools[t].at[pl.ds(b * 2, 2)],
                bsend.at[t, 0], brecv.at[t, 0], device_id=(to, e), device_id_type=MESH,
            ).start()
            return 0

        lax.fori_loop(1, NB, one, 0)
        local(st_a.at[t, :, :, pl.ds(pl.multiple_of(b * kc, kc), kc)], pools[t].at[pl.ds(b * 2, 2)])

    def send_b(t):
        def one(k, _):
            to = lax.rem(b + k, NB)
            pltpu.make_async_remote_copy(
                st_b.at[t, pl.ds(to * 2, 2)],
                landing[t].at[pl.ds(SLOTS, 2), :, pl.ds(pl.multiple_of(b * kc, kc), kc)],
                bsend.at[t, 1], brecv.at[t, 1], device_id=(to, e), device_id_type=MESH,
            ).start()
            return 0

        lax.fori_loop(1, NB, one, 0)
        local(
            st_b.at[t, pl.ds(b * 2, 2)],
            landing[t].at[pl.ds(SLOTS, 2), :, pl.ds(pl.multiple_of(b * kc, kc), kc)],
        )

    send_a(0)
    send_a(1)

    for r in range(SLOTS):
        cvx[r] = to16(cache[r]).astype(BF16)
    own_s = iota((SLOTS * HEADS, BEAM * 0 + 64), 0) // (HEADS * BEAM)
    key_i = iota((SLOTS * HEADS, 64), 1)
    limit = jnp.where(own_s == 0, lens[0, 0], lens[0, 1])
    cross_valid = (key_i // 32 == own_s) & (key_i % 32 < limit)
    enc_k = enc[:, :, :d].reshape(64, d)
    enc_v = enc[:, :, d:].reshape(64, d)
    for t in range(STEPS):
        cross_s[t] = attend(cross_q[t].astype(F32), enc_k, enc_v, cross_valid)

    lane = iota((ROWS, slots), 1)
    expert = lane // PER * 2 + lane % PER // CAP
    place = (lane % CAP).astype(F32)
    earlier = jnp.where(iota((ROWS, ROWS), 1) < iota((ROWS, ROWS), 0), 1.0, 0.0).astype(BF16)
    for t in range(STEPS):
        first = jnp.where(ids[t, :, 0:1] == expert, 1.0, 0.0)
        second = jnp.where(ids[t, :, 1:2] == expert, 1.0, 0.0)
        named = first + second
        rank = jnp.dot(earlier, named.astype(BF16), preferred_element_type=F32)
        chosen = jnp.where(rank == place, named, 0.0)
        pack_p[t] = jnp.transpose(chosen).astype(BF16)
        weight = chosen * (first * gates[t, :, 0:1] + second * gates[t, :, 1:2])
        high = weight.astype(BF16)
        gate_hi[t] = high
        gate_lo[t] = (weight - high.astype(F32)).astype(BF16)

    def stage_b(t):
        for m in range(2 * NB):
            if t == 0:
                st_b[0, m] = pool0[tbl[5, m]]
            else:
                at = tbl[6, m]
                old = pool0[jnp.minimum(at, 15)].astype(F32)
                new = pool1[jnp.maximum(at - 16, 0)].astype(F32)
                entry = pool1[tbl[7, m]].astype(F32)
                kept = jnp.where(iota((POS, kc), 0) * 0 + at < 16, old, new)
                st_b[1, m] = jnp.where(iota((POS, kc), 0) == 14, entry, kept).astype(BF16)

    for t in range(STEPS):
        wait_bytes(pools[t].at[pl.ds(0, 14)], brecv.at[t, 0])
        stage_b(t)
        send_b(t)

    own_r = iota((SLOTS * HEADS, SLOTS * POS), 0) // HEADS
    self_key = iota((SLOTS * HEADS, SLOTS * POS), 1)

    def attention(t):
        wait_bytes(st_b.at[t, pl.ds(0, 14)], brecv.at[t, 1])
        if t == 0:
            for r in range(SLOTS):
                row = cvx[tbl[0, b * SLOTS + r]].astype(F32)
                entry = jnp.broadcast_to(freshf[0, r], (POS, 2 * d))
                ebuf[r] = jnp.where(position == 14, entry, row).astype(BF16)
            held = ebuf
        else:
            for r in range(SLOTS):
                row = ebuf[tbl[1, b * SLOTS + r]].astype(F32)
                entry = jnp.broadcast_to(freshf[1, r], (POS, 2 * d))
                ext1[r] = jnp.where(position == 15, entry, row).astype(BF16)
            held = ext1
            pltpu.make_async_copy(ext1, cache_out, csem).start()
        valid = (self_key // POS == own_r) & (self_key % POS < 15 + t)
        keys = held[0:SLOTS, :, :d].reshape(SLOTS * POS, d)
        values = held[0:SLOTS, :, d:].reshape(SLOTS * POS, d)
        state = (
            layer_in[t].astype(F32)
            + attend(queries[t].astype(F32), keys, values, valid)
            + cross_s[t]
        )
        resid[t] = state
        centered = state - jnp.mean(state, axis=1, keepdims=True)
        variance = jnp.mean(centered * centered, axis=1, keepdims=True)
        normed = centered * lax.rsqrt(variance + 1e-05) * gain[...].astype(F32)
        for j in range(NB):
            hsend[t, j] = normed[:, j * mc : (j + 1) * mc]

        def one(k, _):
            to = lax.rem(b + k, NB)
            pltpu.make_async_remote_copy(
                hsend.at[t, to], hrecv.at[t, b],
                bsend.at[t, 2], brecv.at[t, 2], device_id=(to, e), device_id_type=MESH,
            ).start()
            return 0

        lax.fori_loop(1, NB, one, 0)
        hrecv[t, b] = hsend[t, b]

    half = mc // 2

    def halves(x):
        left = x[:, :half].reshape(ne, PER, half)
        right = x[:, half:].reshape(ne, PER, half)
        return jnp.concatenate([left, right], axis=1).astype(BF16)

    def whole(x):
        x = x.astype(F32)
        left = x[:, :PER].reshape(slots, half)
        right = x[:, PER:].reshape(slots, half)
        return jnp.concatenate([left, right], axis=1).astype(BF16)

    def dispatch(t):
        wait_bytes(hrecv.at[t, pl.ds(0, 7)], brecv.at[t, 2])
        rows = hrecv[t].reshape(ROWS, mc).astype(BF16)
        psend[t] = halves(jnp.dot(pack_p[t], rows, preferred_element_type=F32))

        def one(k, _):
            to = lax.rem(e + k, ne)
            pltpu.make_async_remote_copy(
                psend.at[t, to], xb.at[t, b, e],
                bsend.at[t, 3], brecv.at[t, 3], device_id=(b, to), device_id_type=MESH,
            ).start()
            return 0

        lax.fori_loop(1, ne, one, 0)
        xb[t, b, e] = psend[t, e]

    def ag_copy(t, which, block, to):
        return pltpu.make_async_remote_copy(
            xb.at[t, block], xb.at[t, block],
            agsend.at[t, which], agrecv.at[t, which], device_id=(to, e), device_id_type=MESH,
        )

    def gather_start(t):
        wait_bytes(psend.at[t, pl.ds(0, ne - 1)], brecv.at[t, 3])
        for q in (1, 3, 2):
            ag_copy(t, q, b, peer_y(q) * 2 + c).start()
        ag_copy(t, 0, b, sib).start()

    def up_part(t, block, first):
        x = whole(xb[t, block])
        at = pl.ds(pl.multiple_of(block * mc, mc), mc)
        for k in range(2):
            part = jnp.dot(x, wup[k, at, :], preferred_element_type=F32)
            if first:
                hid[k] = part
            else:
                hid[k] += part

    def gather_compute(t):
        up_part(t, b, True)
        for q in (1, 3, 2):
            block = peer_y(4 - q) * 2 + c
            ag_copy(t, q, block, sib).wait_recv()
            ag_copy(t, 3 + q, block, sib).start()
            if q == 1:
                ag_copy(t, 0, sib, sib).wait_recv()
                up_part(t, sib, False)
            up_part(t, block, False)
        for q in (1, 3, 2):
            block = peer_y(4 - q) * 2 + (1 - c)
            ag_copy(t, 3 + q, block, sib).wait_recv()
            up_part(t, block, False)

    def down_part(t, block, acts):
        at = pl.ds(pl.multiple_of(block * mc, mc), mc)
        return jnp.dot(acts[0], wdn[0, :, at], preferred_element_type=F32) + jnp.dot(
            acts[1], wdn[1, :, at], preferred_element_type=F32
        )

    def sib_copy(t, q):
        return pltpu.make_async_remote_copy(
            sib_s.at[t, q], sib_r.at[t, q],
            sibsend.at[t, q], sibrecv.at[t, q], device_id=(sib, e), device_id_type=MESH,
        )

    def y_copy(t, q):
        return pltpu.make_async_remote_copy(
            ysend.at[t, q - 1], yrecv.at[t, q - 1],
            sibsend.at[t, 3 + q], sibrecv.at[t, 3 + q],
            device_id=(peer_y(q) * 2 + c, e), device_id_type=MESH,
        )

    def scatter_start(t):
        own = iota((slots, hid.shape[2]), 0) % PER // CAP
        acts = [
            jnp.where(own == k, jnp.maximum(hid[k], 0.0), 0.0).astype(BF16) for k in range(2)
        ]
        for q in (1, 3, 2, 0):
            sib_s[t, q] = down_part(t, peer_y(q) * 2 + (1 - c), acts)
            sib_copy(t, q).start()
        for q in (1, 3, 2):
            part = down_part(t, peer_y(q) * 2 + c, acts)
            sib_copy(t, q).wait_recv()
            ysend[t, q - 1] = (part + sib_r[t, q]).astype(BF16)
            y_copy(t, q).start()
        part = down_part(t, b, acts)
        sib_copy(t, 0).wait_recv()
        sib_r[t, 0] = part + sib_r[t, 0]

    def give_back(t):
        total = sib_r[t, 0]
        for q in (1, 3, 2):
            y_copy(t, q).wait_recv()
            total = total + yrecv[t, q - 1].astype(F32)
        rsend[t] = halves(total)

        def one(k, _):
            to = lax.rem(e + k, ne)
            pltpu.make_async_remote_copy(
                rsend.at[t, to], rrecv.at[t, e],
                bsend.at[t, 4], brecv.at[t, 4], device_id=(b, to), device_id_type=MESH,
            ).start()
            return 0

        lax.fori_loop(1, ne, one, 0)
        rrecv[t, e] = rsend[t, e]

    def combine(t):
        wait_bytes(rsend.at[t, pl.ds(0, ne - 1)], brecv.at[t, 4])
        came = whole(rrecv[t])
        mixed = jnp.dot(gate_hi[t], came, preferred_element_type=F32) + jnp.dot(
            gate_lo[t], came, preferred_element_type=F32
        )
        fsend[t] = mixed.reshape(NB, SLOTS, mc)

        def one(k, _):
            to = lax.rem(b + k, NB)
            pltpu.make_async_remote_copy(
                fsend.at[t, to], frecv.at[t, b],
                bsend.at[t, 5], brecv.at[t, 5], device_id=(to, e), device_id_type=MESH,
            ).start()
            return 0

        lax.fori_loop(1, NB, one, 0)
        frecv[t, b] = fsend[t, b]

    def finish(t):
        wait_bytes(frecv.at[t, pl.ds(0, 7)], brecv.at[t, 5])
        for j in range(NB):
            cols = slice(j * mc, (j + 1) * mc)
            layer_out[t, :, cols] = (resid[t, :, cols] + frecv[t, j]).astype(BF16)

    attention(0)
    attention(1)
    dispatch(0)
    dispatch(1)
    gather_start(0)
    up_copy.wait()
    gather_start(1)
    gather_compute(0)
    down_copy.wait()
    scatter_start(0)
    gather_compute(1)
    give_back(0)
    scatter_start(1)
    combine(0)
    give_back(1)
    finish(0)
    combine(1)
    finish(1)

    for t in range(STEPS):
        wait_bytes(st_b.at[t, pl.ds(0, 14)], bsend.at[t, 0])
        wait_bytes(st_b.at[t, pl.ds(0, 14)], bsend.at[t, 1])
        wait_bytes(hsend.at[t, pl.ds(0, 7)], bsend.at[t, 2])
        wait_bytes(psend.at[t, pl.ds(0, ne - 1)], bsend.at[t, 3])
        wait_bytes(rsend.at[t, pl.ds(0, ne - 1)], bsend.at[t, 4])
        wait_bytes(fsend.at[t, pl.ds(0, 7)], bsend.at[t, 5])
        for which in range(7):
            ag_copy(t, which, b, sib).wait_send()
        for q in range(4):
            sib_copy(t, q).wait_send()
        for q in range(1, 4):
            y_copy(t, q).wait_send()
    pltpu.make_async_copy(ext1, cache_out, csem).wait()


def shards(
    layer_in, queries, fresh_entries, cross_queries, past_cache, encoder_states, source_lengths,
    parents, expert_ids, gate_weights, norm_gain, up_weight, down_weight,
):
    ne = lax.axis_size("expert")
    d = HEADS * DH
    mc = d // NB
    half = mc // 2
    kc = 2 * d // NB
    slots = ne * PER
    hs = up_weight.shape[2]
    tables = pl.pallas_call(
        plan_kernel,
        out_shape=jax.ShapeDtypeStruct((8, ROWS), jnp.int32),
        in_specs=[pl.BlockSpec(memory_space=pltpu.VMEM)],
        out_specs=pl.BlockSpec(memory_space=pltpu.VMEM),
        name="plan",
    )(parents[:, 0])
    vmem = pl.BlockSpec(memory_space=pltpu.VMEM)
    smem = pl.BlockSpec(memory_space=pltpu.SMEM)
    hbm = pl.BlockSpec(memory_space=pl.ANY)
    dma = pltpu.SemaphoreType.DMA
    layer_out, cache_out = pl.pallas_call(
        functools.partial(layer_kernel, ne),
        out_shape=(
            jax.ShapeDtypeStruct((STEPS, SLOTS, d), BF16),
            jax.ShapeDtypeStruct((SLOTS, POS, 2 * d), BF16),
        ),
        in_specs=[smem, smem] + [vmem] * 9 + [hbm, hbm],
        out_specs=(vmem, hbm),
        scratch_shapes=[
            pltpu.VMEM((2, d, hs), BF16),
            pltpu.VMEM((2, hs, d), BF16),
            pltpu.VMEM((STEPS, SLOTS, 1, 2 * d), F32),
            pltpu.VMEM((STEPS, 2, POS, 2 * d), BF16),
            pltpu.VMEM((16, POS, kc), BF16),
            pltpu.VMEM((16, POS, kc), BF16),
            pltpu.VMEM((STEPS, 16, POS, kc), BF16),
            pltpu.VMEM((SLOTS + 2, POS, 2 * d), BF16),
            pltpu.VMEM((SLOTS + 2, POS, 2 * d), BF16),
            pltpu.VMEM((SLOTS, POS, 2 * d), BF16),
            pltpu.VMEM((STEPS, SLOTS, d), F32),
            pltpu.VMEM((STEPS, SLOTS, d), F32),
            pltpu.VMEM((STEPS, slots, ROWS), BF16),
            pltpu.VMEM((STEPS, ROWS, slots), BF16),
            pltpu.VMEM((STEPS, ROWS, slots), BF16),
            pltpu.VMEM((STEPS, NB, SLOTS, mc), F32),
            pltpu.VMEM((STEPS, NB, SLOTS, mc), F32),
            pltpu.VMEM((STEPS, ne, 2 * PER, half), BF16),
            pltpu.VMEM((STEPS, NB, ne, 2 * PER, half), BF16),
            pltpu.VMEM((2, slots, hs), F32),
            pltpu.VMEM((STEPS, 4, slots, mc), F32),
            pltpu.VMEM((STEPS, 4, slots, mc), F32),
            pltpu.VMEM((STEPS, 3, slots, mc), BF16),
            pltpu.VMEM((STEPS, 3, slots, mc), BF16),
            pltpu.VMEM((STEPS, ne, 2 * PER, half), BF16),
            pltpu.VMEM((STEPS, ne, 2 * PER, half), BF16),
            pltpu.VMEM((STEPS, NB, SLOTS, mc), F32),
            pltpu.VMEM((STEPS, NB, SLOTS, mc), F32),
            dma((2,)),
            dma,
            dma,
            dma((STEPS, 6)),
            dma((STEPS, 6)),
            dma((STEPS, 7)),
            dma((STEPS, 7)),
            dma((STEPS, 7)),
            dma((STEPS, 7)),
        ],
        compiler_params=pltpu.CompilerParams(
            collective_id=1, has_side_effects=True, vmem_limit_bytes=56 * 2**20
        ),
        cost_estimate=pl.CostEstimate(
            flops=4 * STEPS * slots * d * hs * 2, bytes_accessed=12 * 2**20, transcendentals=0
        ),
        name="layer",
    )(
        tables, source_lengths, layer_in[:, 0], queries[:, 0], fresh_entries[:, 0],
        cross_queries[:, 0], past_cache[0], encoder_states[0], expert_ids[:, 0],
        gate_weights[:, 0], norm_gain[None], up_weight, down_weight,
    )
    return layer_out[:, None], cache_out[None]


def solution(mesh):
    in_specs = (
        P(None, "expert", "batch", None),
        P(None, "expert", "batch", None),
        P(None, "expert", "batch", None),
        P(None, "expert", "batch", None),
        P("expert", "batch", None, None),
        P("expert", "batch", None, None),
        P("expert", "batch"),
        P(None, "expert", None),
        P(None, "expert", None, None),
        P(None, "expert", None, None),
        P(),
        P("expert", None, "batch"),
        P("expert", "batch", None),
    )
    out_specs = (P(None, "expert", "batch", None), P("expert", "batch", None, None))
    return jax.shard_map(shards, mesh=mesh, in_specs=in_specs, out_specs=out_specs, check_vma=False)
```

time: 333 us -> 96.4 us (0.29)
  waiting for transfers between devices: 170 us -> 0 us
  Pallas kernels: 0 us -> 84.9 us
  local copies, waits for them, and re-layouts: 46.6 us -> 10.5 us
  starting transfers between devices: 30.1 us -> 0 us
  blocking collectives: 26.2 us -> 0 us
  other arithmetic: 24.9 us -> 0 us
  matrix products: 17.2 us -> 0 us
  between operations: 14.5 us -> 0.64 us
    all_to_all x4 -> x0, waiting for transfers between devices: 93.6 us -> none  [the longest x2 64.3 us: expert_mix(): lax.all_to_all(expert_out, 'expert', split_axis=0, concat_axis=0, tiled=T...]
    pallas_call x0 -> x2, Pallas kernels: none -> 84.9 us  [the longest x1 83.2 us: shards(): pl.pallas_call(functools.partial(layer_kernel, ne), out_shape=(jax.ShapeD...]
    all_gather x2 -> x0, waiting for transfers between devices: 46.4 us -> none  [reorder(): arrived = lax.all_gather(cache_rows[picked], 'batch', axis=0, tiled=True)]
    reduce_scatter x2 -> x0, waiting for transfers between devices: 30.2 us -> none  [expert_mix(): lax.psum_scatter(weighted.reshape(sections, group_rows, model_width), 'ba...]
    all_to_all x4 -> x0, starting transfers between devices: 29.7 us -> none  [the longest x2 15.7 us: expert_mix(): lax.all_to_all(packed, 'expert', split_axis=0, concat_axis=0, tiled=True)]
    all_gather x2 -> x0, blocking collectives: 26.2 us -> none  [expert_mix(): gathered = lax.all_gather(normed, 'batch', axis=1, tiled=True)]
    dot_general x12 -> x0, matrix products: 17.2 us -> none  [the longest x2 12.5 us: expert_mix(): jnp.einsum('nxch,xhd->nxcd', inner_act, down_weight, preferred_element_ty...]
    gather x10 -> x0, local copies, waits for them, and re-layouts: 16.7 us -> none  [the longest x4 7.56 us: expert_mix(): picked = returned[slot_ids]]
  transfers between devices with their start and end apart: 8 -> 0, of which waited for: 7 -> 0; matrix products, arithmetic and copies ran while one was open for 19% -> 0% of each run, Pallas kernels for 0% -> 0%
where the time goes in v1:
time: 96.4 us; the launch traced here: 96 us
  Pallas kernels  84.9 us (88%)
  local copies, waits for them, and re-layouts  10.5 us (11%)
    pallas_call x1, Pallas kernels, shards(): pl.pallas_call(functools.partial(layer_kernel, ne), out_shape=(jax.ShapeD...  83.2 us
    unnamed x5, local copies, waits for them, and re-layouts  9.25 us

profile of v1, /device:TPU:1, one launch (start us, length us, event | category | flops | bytes accessed | tf_op | source)
XLA Modules:
  0.0 96.0 jit_solution(15340860361040232505)
XLA Ops:
  0.6 1.7 %plan.1.tbl = s32[8,64]{1,0:T(8,128)} custom-call(s32[2,64]{1,0:T(2,128)} %bitcast.20), custom_call_target="tpu_custom_call" | custom-call | tf_op jit(solution)/shard_map/plan/pallas_call | solution.py:487
  2.3 1.3 %broadcast_in_dim.9.gain = bf16[1,2048]{1,0:T(2,128)(2,1)} reshape(bf16[2048]{0:T(1024)(128)(2,1)} %param.23) | data formatting | bytes 8192 | tf_op jit(solution)/shard_map/broadcast_in_dim | solution.py:555
  3.6 1.4 %copy.16 = s32[2,1,64,2]{3,2,0,1:T(8,128)} copy(s32[2,1,64,2]{2,3,1,0:T(2,128)} %param.21) | data formatting | bytes 2048 | tf_op args[8]
  5.0 1.4 %copy.17 = f32[2,1,64,2]{3,2,0,1:T(8,128)} copy(f32[2,1,64,2]{2,3,1,0:T(2,128)} %param.22) | data formatting | bytes 2048 | tf_op args[9]
  6.4 2.7 %copy.20 = bf16[1,8,14,4096]{3,2,1,0:T(8,128)(2,1)} copy(bf16[1,8,14,4096]{3,1,2,0:T(8,128)(2,1)} %param.17) | data formatting | bytes 1835008 | tf_op args[4]
  9.1 83.2 %layer.1 = (bf16[2,8,2048]{2,1,0:T(8,128)(2,1)}, bf16[8,16,4096]{2,1,0:T(8,128)(2,1)}) custom-call(s32[8,64]{1,0:T(8,128)} %plan.1.tbl, s32[1,2]{1,0:T(1,128)} %lens.1, bf16[2,8,2048]{2,1,0:T(8,128)(2,1)} %bitcast.23, bf16[2,8,2048]{2,1,0:T(8,128)(2,1)} %bitcast.24, bf16[2,8,4096]{2,1,0:T(8,128)(2,1)} %bitcast.22, bf16[2,8,2048]{2,1,0:T(8,128)(2,1)} %bitcast.25, ...), custom_call_target="tpu_custom_call" | custom-call | flops 4294967296 | bytes 12582912 | tf_op jit(solution)/shard_map/layer/pallas_call | solution.py:498
  92.3 1.5 %copy.23 = bf16[2,1,8,2048]{3,2,1,0:T(8,128)(2,1)} copy(bf16[2,1,8,2048]{3,2,1,0:T(8,128)(2,1)} %bitcast.17) | data formatting | bytes 131072
  93.8 2.3 %copy.24 = bf16[1,8,16,4096]{3,2,1,0:T(8,128)(2,1)} copy(bf16[1,8,16,4096]{3,2,1,0:T(8,128)(2,1)} %bitcast.15) | data formatting | bytes 2097152

commit v2 on v1

v2 whole, which is shorter than its diff:
```python
import functools

import jax
import jax.numpy as jnp
from jax import lax
from jax.experimental import pallas as pl
from jax.experimental.pallas import tpu as pltpu
from jax.sharding import PartitionSpec as P

HEADS = 16
DH = 128
CAP = 4
STEPS = 2
SLOTS = 8
BEAM = 4
CACHE = 14
NB = 8
ROWS = NB * SLOTS
PER = 2 * CAP
POS = 16
MESH = pl.DeviceIdType.MESH
F32 = jnp.float32
BF16 = jnp.bfloat16


def iota(shape, dim):
    return lax.broadcasted_iota(jnp.int32, shape, dim)


def hot(mask):
    return jnp.where(mask, 1.0, 0.0).astype(BF16)


def dot(x, y):
    return jnp.dot(x, y, preferred_element_type=F32)


def move_plan(par):
    n = ROWS
    row, col = iota((n, n), 1), iota((n, n), 0)
    dev_r, dev_c = row // SLOTS, col // SLOTS
    before = jnp.where((row < col) & (dev_r == dev_c), 1.0, 0.0)

    def across(x):
        return jnp.broadcast_to(jnp.sum(x, axis=1, keepdims=True), (n, n))

    def down(x):
        return jnp.broadcast_to(jnp.sum(x, axis=0, keepdims=True), (n, n))

    eye = jnp.where(row == col, 1.0, 0.0)
    par_r = jnp.broadcast_to(par, (n, n))
    takes = jnp.where(col == par_r, 1.0, 0.0)
    cross_r = jnp.where(par_r // SLOTS != dev_r, 1.0, 0.0)
    cross_c = across(eye * cross_r)
    leave_c = across(takes * cross_r)
    leave_r = down(eye * leave_c)
    give_c = across(before * leave_r) + 2.0 * dev_c.astype(F32)
    give_r = down(eye * give_c)
    take_c = across(before * cross_r) + 2.0 * dev_c.astype(F32)
    take_r = down(eye * take_c)
    rowf, colf = row.astype(F32), col.astype(F32)
    given = jnp.where(rowf == give_c, leave_c, 0.0).astype(BF16)
    given_t = jnp.where(colf == give_r, leave_r, 0.0).astype(BF16)
    taken = jnp.where(rowf == take_c, cross_c, 0.0).astype(BF16)
    taken_t = jnp.where(colf == take_r, cross_r, 0.0).astype(BF16)
    takes_t = jnp.transpose(takes).astype(BF16)
    return takes_t, given, given_t, taken, taken_t


def head_mask(rows):
    head = iota((rows, HEADS, HEADS * DH), 1)
    column = iota((rows, HEADS, HEADS * DH), 2) // DH
    return (head == column).astype(F32)


def attend(q, keys, values, valid):
    d = HEADS * DH
    mask = head_mask(SLOTS)
    spread = (jnp.broadcast_to(q[:, None, :], (SLOTS, HEADS, d)) * mask).reshape(SLOTS * HEADS, d)
    scores = lax.dot_general(
        spread.astype(BF16), keys, (((1,), (1,)), ((), ())), preferred_element_type=F32
    ) * (1.0 / DH**0.5)
    scores = jnp.where(valid, scores, -1e30)
    raised = jnp.where(valid, jnp.exp(scores - jnp.max(scores, axis=1, keepdims=True)), 0.0)
    weights = (raised / jnp.sum(raised, axis=1, keepdims=True)).astype(BF16)
    out = jnp.dot(weights, values, preferred_element_type=F32)
    return jnp.sum(out.reshape(SLOTS, HEADS, d) * mask, axis=1)


def layer_kernel(
    ne,
    lens, par, layer_in, queries, fresh, cross_q, cache, enc, ids, gates, gain, up_hbm, down_hbm,
    layer_out, cache_out,
    wup, wdn, src0, src1, ext1, st_a, pool0, pool1, st_b, cross_s, resid,
    pack_p, gate_hi, gate_lo, hsend, hrecv, psend, xb, hid, sib_s, sib_r, ysend, yrecv,
    rsend, rrecv, fsend, frecv, wsem, lsem, csem, bsend, brecv, agsend, agrecv, sibsend, sibrecv,
):
    b, e = lax.axis_index("batch"), lax.axis_index("expert")
    y, c = b // 2, b % 2
    sib = y * 2 + (1 - c)
    d = HEADS * DH
    kc = 2 * d // NB
    mc = d // NB
    slots = ne * PER
    unsent, unreceived = [], {}

    def peer_y(q):
        return lax.rem(y + q, 4)

    barrier = pltpu.get_barrier_semaphore()

    def greet_b(k, _):
        pl.semaphore_signal(
            barrier, inc=1, device_id=(lax.rem(b + k, NB), e), device_id_type=MESH
        )
        return 0

    def greet_e(k, _):
        pl.semaphore_signal(
            barrier, inc=1, device_id=(b, lax.rem(e + k, ne)), device_id_type=MESH
        )
        return 0

    lax.fori_loop(1, NB, greet_b, 0)
    lax.fori_loop(1, ne, greet_e, 0)

    up_copy = pltpu.make_async_copy(up_hbm, wup, wsem.at[0])
    down_copy = pltpu.make_async_copy(down_hbm, wdn, wsem.at[1])
    up_copy.start()
    down_copy.start()

    def local(src, dst):
        copy = pltpu.make_async_copy(src, dst, lsem)
        copy.start()
        copy.wait()

    def wait_bytes(ref, sem):
        pltpu.make_async_copy(ref, ref, sem).wait()

    def to_all(axis, t, phase, make, ref):
        count = NB if axis == "batch" else ne

        def one(k, _):
            src, dst, to = make(k)
            to = (to, e) if axis == "batch" else (b, to)
            pltpu.make_async_remote_copy(
                src, dst, bsend.at[t, phase], brecv.at[t, phase], device_id=to, device_id_type=MESH
            ).start()
            return 0

        lax.fori_loop(1, count, one, 0)
        unsent.append(lambda: wait_bytes(ref, bsend.at[t, phase]))
        unreceived[t, phase] = lambda: wait_bytes(ref, brecv.at[t, phase])

    def arrive(t, phase):
        unreceived.pop((t, phase))()

    near, late = CACHE * SLOTS, CACHE * SLOTS + 2 * POS
    src0[0:near] = cache[...].astype(F32).reshape(near, 2 * d).astype(BF16)
    blank = jnp.zeros((SLOTS, 2 * d), F32)
    src0[late:] = jnp.concatenate([fresh[0].astype(F32), blank], axis=0).astype(BF16)
    src1[late + POS :] = jnp.concatenate([fresh[1].astype(F32), blank], axis=0).astype(BF16)

    same_dev = iota((ROWS, ROWS), 0) // SLOTS == iota((ROWS, ROWS), 1) // SLOTS
    own_m = hot(iota((2 * POS, ROWS), 1) == 2 * b + iota((2 * POS, ROWS), 0) // POS)
    near_c = hot(iota((ROWS, near), 0) == SLOTS * b + iota((ROWS, near), 1) % SLOTS)
    near_p = iota((2 * POS, near), 0) % POS == iota((2 * POS, near), 1) // SLOTS

    def given_rows(chosen):
        pick = dot(dot(own_m, chosen).astype(BF16), near_c)
        return dot(jnp.where(near_p, pick, 0.0).astype(BF16), src0[0:near])

    takes0, given0, given0_t, taken0, taken0_t = move_plan(par[0:1, :])
    st_a[0] = given_rows(given0_t).astype(BF16)

    pl.semaphore_wait(barrier, NB - 1 + ne - 1)

    pools = (pool0, pool1)

    def own_cols(k):
        return pl.ds(pl.multiple_of(k * kc, kc), kc)

    def own_rows(k):
        return pl.ds(pl.multiple_of(k * 2 * POS, 2 * POS), 2 * POS)

    def send_a(t):
        def make(k):
            to = lax.rem(b + k, NB)
            return st_a.at[t, :, own_cols(to)], pools[t].at[own_rows(b)], to

        to_all("batch", t, 0, make, st_b.at[t, pl.ds(0, 14 * POS)])
        local(st_a.at[t, :, own_cols(b)], pools[t].at[own_rows(b)])

    def send_b(t):
        landing = src0.at[near:late] if t == 0 else src1.at[SLOTS * POS : SLOTS * POS + 2 * POS]

        def make(k):
            to = lax.rem(b + k, NB)
            return st_b.at[t, own_rows(to)], landing.at[:, own_cols(b)], to

        to_all("batch", t, 1, make, st_b.at[t, pl.ds(0, 14 * POS)])
        local(st_b.at[t, own_rows(b)], landing.at[:, own_cols(b)])

    send_a(0)

    takes1, given1, given1_t, taken1, taken1_t = move_plan(par[1:2, :])
    kept1_t = dot(given1_t, jnp.where(same_dev, takes0.astype(F32), 0.0).astype(BF16)).astype(BF16)
    slot_c = hot(
        (iota((ROWS, POS), 0) == SLOTS * b + iota((ROWS, POS), 1)) & (iota((ROWS, POS), 1) < SLOTS)
    )
    entry = dot(dot(own_m, given1_t).astype(BF16), slot_c)
    entry = jnp.where(iota((2 * POS, POS), 0) % POS == CACHE, entry, 0.0).astype(BF16)
    st_a[1] = (given_rows(kept1_t) + dot(entry, src0[late:])).astype(BF16)

    own_s = iota((SLOTS * HEADS, 64), 0) // (HEADS * BEAM)
    key_i = iota((SLOTS * HEADS, 64), 1)
    limit = jnp.where(own_s == 0, lens[0, 0], lens[0, 1])
    cross_valid = (key_i // 32 == own_s) & (key_i % 32 < limit)
    enc_k = enc[:, :, :d].reshape(64, d)
    enc_v = enc[:, :, d:].reshape(64, d)

    def cross(t):
        cross_s[t] = attend(cross_q[t].astype(F32), enc_k, enc_v, cross_valid)

    def route(t):
        slot = iota((slots, ROWS), 0)
        owner = lax.rem(slot // PER + e, ne)
        expert = owner * 2 + slot % PER // CAP
        earlier = hot(iota((ROWS, ROWS), 0) < iota((ROWS, ROWS), 1))
        first = jnp.where(ids[t, 0:1, :] == expert, 1.0, 0.0)
        second = jnp.where(ids[t, 1:2, :] == expert, 1.0, 0.0)
        named = first + second
        rank = dot(named.astype(BF16), earlier)
        chosen = jnp.where(rank == (slot % CAP).astype(F32), named, 0.0)
        pack_p[t] = chosen.astype(BF16)
        weight = chosen * (first * gates[t, 0:1, :] + second * gates[t, 1:2, :])
        weight = jnp.transpose(weight)
        high = weight.astype(BF16)
        gate_hi[t] = high
        gate_lo[t] = (weight - high.astype(F32)).astype(BF16)

    pairs = 2 * NB * POS
    pair_m = hot(iota((pairs, ROWS), 0) // POS == iota((pairs, ROWS), 1))
    pair_mt = hot(iota((ROWS, pairs), 0) == iota((ROWS, pairs), 1) // POS)
    same_p = iota((pairs, pairs), 0) % POS == iota((pairs, pairs), 1) % POS

    def spread(small):
        wide = dot(dot(pair_m, small.astype(BF16)).astype(BF16), pair_mt)
        return jnp.where(same_p, wide, 0.0).astype(BF16)

    from0 = dot(takes0, given0).astype(BF16)
    hand0 = spread(dot(taken0_t, from0))

    def select(t, takes, taken):
        held = near if t == 0 else SLOTS * POS
        width = held + 2 * POS + POS
        shape = (SLOTS * POS, width)
        k, out_p, out_r = iota(shape, 1), iota(shape, 0) % POS, iota(shape, 0) // POS
        own_r = hot(
            iota((SLOTS * POS, ROWS), 1) == SLOTS * b + iota((SLOTS * POS, ROWS), 0) // POS
        )
        kk, cc = iota((ROWS, width), 1), iota((ROWS, width), 0)
        slot = kk % SLOTS if t == 0 else kk // POS
        at_c = hot((kk < held) & (cc == SLOTS * b + slot))
        at_m = hot((kk >= held) & (kk < held + 2 * POS) & (cc == 2 * b + (kk - held) // POS))
        picked = dot(dot(own_r, takes).astype(BF16), at_c)
        picked = picked + dot(dot(own_r, taken).astype(BF16), at_m)
        old_p = k // SLOTS if t == 0 else k % POS
        key_p = jnp.where(k < held, old_p, (k - held) % POS)
        picked = jnp.where((key_p == out_p) & (k < held + 2 * POS), picked, 0.0)
        new = (k - (held + 2 * POS) == out_r) & (out_p == CACHE + t)
        return jnp.where(new, 1.0, picked).astype(BF16)

    via1 = dot(taken1_t, takes1).astype(BF16)
    arrive(0, 0)
    st_b[0] = dot(hand0, pool0[...]).astype(BF16)
    send_b(0)
    send_a(1)
    hand1_old = spread(dot(via1, from0))
    hand1_new = spread(dot(via1, given1))
    select0 = select(0, takes0, taken0)
    cross(0)

    own_r = iota((SLOTS * HEADS, SLOTS * POS), 0) // HEADS
    self_key = iota((SLOTS * HEADS, SLOTS * POS), 1)

    def attention(t):
        arrive(t, 1)
        if t == 0:
            src1[0 : SLOTS * POS] = dot(select0, src0[...]).astype(BF16)
            held = src1
        else:
            ext1[...] = dot(select1, src1[...]).astype(BF16)
            held = ext1
            pltpu.make_async_copy(ext1, cache_out, csem).start()
            unsent.append(lambda: pltpu.make_async_copy(ext1, cache_out, csem).wait())
        valid = (self_key // POS == own_r) & (self_key % POS < CACHE + 1 + t)
        keys = held[0 : SLOTS * POS, :d]
        values = held[0 : SLOTS * POS, d:]
        state = (
            layer_in[t].astype(F32)
            + attend(queries[t].astype(F32), keys, values, valid)
            + cross_s[t]
        )
        resid[t] = state
        centered = state - jnp.mean(state, axis=1, keepdims=True)
        variance = jnp.mean(centered * centered, axis=1, keepdims=True)
        gains = gain[...].astype(F32).reshape(1, d)
        normed = centered * lax.rsqrt(variance + 1e-05) * gains
        for j in range(NB):
            hsend[t, j] = normed[:, j * mc : (j + 1) * mc]

        def make(k):
            to = lax.rem(b + k, NB)
            return hsend.at[t, to], hrecv.at[t, b], to

        to_all("batch", t, 2, make, hsend.at[t, pl.ds(0, NB - 1)])
        hrecv[t, b] = hsend[t, b]

    half = mc // 2

    def halves(x):
        left = x[:, :half].reshape(ne, PER, half)
        right = x[:, half:].reshape(ne, PER, half)
        return jnp.concatenate([left, right], axis=1).astype(BF16)

    def whole(x):
        x = x.astype(F32)
        left = x[:, :PER].reshape(slots, half)
        right = x[:, PER:].reshape(slots, half)
        return jnp.concatenate([left, right], axis=1).astype(BF16)

    def dispatch(t):
        arrive(t, 2)
        rows = hrecv[t].reshape(ROWS, mc).astype(BF16)
        psend[t] = halves(dot(pack_p[t], rows))

        def make(k):
            return psend.at[t, k], xb.at[t, b, k], lax.rem(e + k, ne)

        to_all("expert", t, 3, make, psend.at[t, pl.ds(0, ne - 1)])
        xb[t, b, 0] = psend[t, 0]

    low, high = pl.ds(0, ne // 2), pl.ds(ne // 2, ne // 2)
    every = pl.ds(0, ne)
    up_y, down_y = peer_y(1) * 2, peer_y(3) * 2
    far_y = peer_y(2) * 2

    def ag_copy(t, which):
        block, part, to = (
            (b, every, sib),
            (b, low, up_y + c),
            (b, high, down_y + c),
            (b, high, up_y + c),
            (b, low, down_y + c),
            (down_y + c, low, up_y + c),
            (up_y + c, high, down_y + c),
            (down_y + c, every, sib),
            (up_y + c, every, sib),
            (far_y + c, low, sib),
            (far_y + c, high, sib),
        )[which]
        return pltpu.make_async_remote_copy(
            xb.at[t, block, part], xb.at[t, block, part],
            agsend.at[t, which], agrecv.at[t, which], device_id=(to, e), device_id_type=MESH,
        )

    def gather_start(t):
        arrive(t, 3)
        for which in (1, 2, 3, 4, 0):
            ag_copy(t, which).start()
        for which in range(11):
            unsent.append(lambda which=which: ag_copy(t, which).wait_send())

    def gather_relay(t):
        for came, relay in ((1, 5), (2, 6)):
            ag_copy(t, came).wait_recv()
            ag_copy(t, relay).start()
        for came, pass_on in ((3, 7), (4, 8)):
            ag_copy(t, came).wait_recv()
            ag_copy(t, pass_on).start()

    def up_part(t, block, first):
        x = whole(xb[t, block])
        at = pl.ds(pl.multiple_of(block * mc, mc), mc)
        for k in range(2):
            part = jnp.dot(x, wup[k, at, :], preferred_element_type=F32)
            if first:
                hid[k] = part
            else:
                hid[k] += part

    def gather_compute(t):
        up_part(t, b, True)
        ag_copy(t, 0).wait_recv()
        up_part(t, sib, False)
        up_part(t, down_y + c, False)
        up_part(t, up_y + c, False)
        for came, pass_on in ((5, 9), (6, 10)):
            ag_copy(t, came).wait_recv()
            ag_copy(t, pass_on).start()
        ag_copy(t, 7).wait_recv()
        up_part(t, down_y + 1 - c, False)
        ag_copy(t, 8).wait_recv()
        up_part(t, up_y + 1 - c, False)
        up_part(t, far_y + c, False)
        ag_copy(t, 9).wait_recv()
        ag_copy(t, 10).wait_recv()
        up_part(t, far_y + 1 - c, False)

    def down_part(t, block, acts):
        at = pl.ds(pl.multiple_of(block * mc, mc), mc)
        return jnp.dot(acts[0], wdn[0, :, at], preferred_element_type=F32) + jnp.dot(
            acts[1], wdn[1, :, at], preferred_element_type=F32
        )

    def sib_copy(t, q):
        return pltpu.make_async_remote_copy(
            sib_s.at[t, q], sib_r.at[t, q],
            sibsend.at[t, q], sibrecv.at[t, q], device_id=(sib, e), device_id_type=MESH,
        )

    def y_copy(t, which):
        to = (up_y, down_y, up_y, down_y, up_y, down_y)[which] + c
        return pltpu.make_async_remote_copy(
            ysend.at[t, which], yrecv.at[t, which],
            sibsend.at[t, 4 + which], sibrecv.at[t, 4 + which],
            device_id=(to, e), device_id_type=MESH,
        )

    first, second = slice(0, slots // 2), slice(slots // 2, slots)

    def y_send(t, which, part):
        ysend[t, which] = part.astype(BF16)
        y_copy(t, which).start()

    def scatter_start(t):
        for q in range(4):
            unsent.append(lambda q=q: sib_copy(t, q).wait_send())
        for which in range(6):
            unsent.append(lambda which=which: y_copy(t, which).wait_send())
        own = iota((slots, hid.shape[2]), 0) % PER // CAP
        acts = [
            jnp.where(own == k, jnp.maximum(hid[k], 0.0), 0.0).astype(BF16) for k in range(2)
        ]
        def for_sib(q):
            sib_s[t, q] = down_part(t, peer_y(q) * 2 + (1 - c), acts)
            sib_copy(t, q).start()

        for_sib(2)
        for q, after in ((2, 1), (1, 3), (3, 0), (0, None)):
            if after is not None:
                for_sib(after)
            part = down_part(t, peer_y(q) * 2 + c, acts)
            sib_copy(t, q).wait_recv()
            part = part + sib_r[t, q]
            if q == 2:
                y_send(t, 0, part[first])
                y_send(t, 1, part[second])
            elif q == 1:
                y_send(t, 2, part[second])
                sib_r[t, 1, first] = part[first]
            elif q == 3:
                y_send(t, 3, part[first])
                sib_r[t, 3, second] = part[second]
            else:
                sib_r[t, 0] = part

    def scatter_relay(t):
        y_copy(t, 0).wait_recv()
        y_send(t, 4, sib_r[t, 1, first] + yrecv[t, 0].astype(F32))
        y_copy(t, 1).wait_recv()
        y_send(t, 5, sib_r[t, 3, second] + yrecv[t, 1].astype(F32))

    def give_back(t):
        for which in range(2, 6):
            y_copy(t, which).wait_recv()
        upper = sib_r[t, 0, first] + yrecv[t, 3].astype(F32) + yrecv[t, 4].astype(F32)
        lower = sib_r[t, 0, second] + yrecv[t, 2].astype(F32) + yrecv[t, 5].astype(F32)
        total = jnp.concatenate([upper, lower], axis=0)
        rsend[t] = halves(total)

        def make(k):
            return rsend.at[t, k], rrecv.at[t, k], lax.rem(e - k + ne, ne)

        to_all("expert", t, 4, make, rsend.at[t, pl.ds(0, ne - 1)])
        rrecv[t, 0] = rsend[t, 0]

    def combine(t):
        arrive(t, 4)
        came = whole(rrecv[t])
        mixed = jnp.dot(gate_hi[t], came, preferred_element_type=F32) + jnp.dot(
            gate_lo[t], came, preferred_element_type=F32
        )
        fsend[t] = mixed.reshape(NB, SLOTS, mc)

        def make(k):
            to = lax.rem(b + k, NB)
            return fsend.at[t, to], frecv.at[t, b], to

        to_all("batch", t, 5, make, fsend.at[t, pl.ds(0, NB - 1)])
        frecv[t, b] = fsend[t, b]

    def finish(t):
        arrive(t, 5)
        for j in range(NB):
            cols = slice(j * mc, (j + 1) * mc)
            layer_out[t, :, cols] = (resid[t, :, cols] + frecv[t, j]).astype(BF16)

    attention(0)
    arrive(1, 0)
    st_b[1] = (dot(hand1_old, pool0[...]) + dot(hand1_new, pool1[...])).astype(BF16)
    send_b(1)
    route(0)
    dispatch(0)
    select1 = select(1, takes1, taken1)
    cross(1)
    attention(1)
    route(1)
    gather_start(0)
    dispatch(1)
    up_copy.wait()
    gather_relay(0)
    gather_start(1)
    gather_compute(0)
    down_copy.wait()
    scatter_start(0)
    gather_relay(1)
    scatter_relay(0)
    gather_compute(1)
    scatter_start(1)
    give_back(0)
    scatter_relay(1)
    give_back(1)
    combine(0)
    finish(0)
    combine(1)
    finish(1)

    for done in unsent:
        done()


def emit_kernel(layer_in, cache_in, layer_out, cache_out, sem):
    copies = [
        pltpu.make_async_copy(cache_in, cache_out, sem.at[0]),
        pltpu.make_async_copy(layer_in, layer_out, sem.at[1]),
    ]
    for copy in copies:
        copy.start()
    for copy in copies:
        copy.wait()


def shards(
    layer_in, queries, fresh_entries, cross_queries, past_cache, encoder_states, source_lengths,
    parents, expert_ids, gate_weights, norm_gain, up_weight, down_weight,
):
    ne = lax.axis_size("expert")
    d = HEADS * DH
    mc = d // NB
    half = mc // 2
    kc = 2 * d // NB
    slots = ne * PER
    hs = up_weight.shape[2]
    vmem = pl.BlockSpec(memory_space=pltpu.VMEM)
    smem = pl.BlockSpec(memory_space=pltpu.SMEM)
    hbm = pl.BlockSpec(memory_space=pl.ANY)
    dma = pltpu.SemaphoreType.DMA
    layer_out, cache_out = pl.pallas_call(
        functools.partial(layer_kernel, ne),
        out_shape=(
            jax.ShapeDtypeStruct((STEPS, SLOTS, d), BF16),
            jax.ShapeDtypeStruct((SLOTS * POS, 2 * d), BF16),
        ),
        in_specs=[smem] + [vmem] * 10 + [hbm, hbm],
        out_specs=(vmem, hbm),
        scratch_shapes=[
            pltpu.VMEM((2, d, hs), BF16),
            pltpu.VMEM((2, hs, d), BF16),
            pltpu.VMEM((CACHE * SLOTS + 2 * POS + POS, 2 * d), BF16),
            pltpu.VMEM((SLOTS * POS + 2 * POS + POS, 2 * d), BF16),
            pltpu.VMEM((SLOTS * POS, 2 * d), BF16),
            pltpu.VMEM((STEPS, 2 * POS, 2 * d), BF16),
            pltpu.VMEM((2 * NB * POS, kc), BF16),
            pltpu.VMEM((2 * NB * POS, kc), BF16),
            pltpu.VMEM((STEPS, 2 * NB * POS, kc), BF16),
            pltpu.VMEM((STEPS, SLOTS, d), F32),
            pltpu.VMEM((STEPS, SLOTS, d), F32),
            pltpu.VMEM((STEPS, slots, ROWS), BF16),
            pltpu.VMEM((STEPS, ROWS, slots), BF16),
            pltpu.VMEM((STEPS, ROWS, slots), BF16),
            pltpu.VMEM((STEPS, NB, SLOTS, mc), F32),
            pltpu.VMEM((STEPS, NB, SLOTS, mc), F32),
            pltpu.VMEM((STEPS, ne, 2 * PER, half), BF16),
            pltpu.VMEM((STEPS, NB, ne, 2 * PER, half), BF16),
            pltpu.VMEM((2, slots, hs), F32),
            pltpu.VMEM((STEPS, 4, slots, mc), F32),
            pltpu.VMEM((STEPS, 4, slots, mc), F32),
            pltpu.VMEM((STEPS, 6, slots // 2, mc), BF16),
            pltpu.VMEM((STEPS, 6, slots // 2, mc), BF16),
            pltpu.VMEM((STEPS, ne, 2 * PER, half), BF16),
            pltpu.VMEM((STEPS, ne, 2 * PER, half), BF16),
            pltpu.VMEM((STEPS, NB, SLOTS, mc), F32),
            pltpu.VMEM((STEPS, NB, SLOTS, mc), F32),
            dma((2,)),
            dma,
            dma,
            dma((STEPS, 6)),
            dma((STEPS, 6)),
            dma((STEPS, 11)),
            dma((STEPS, 11)),
            dma((STEPS, 10)),
            dma((STEPS, 10)),
        ],
        compiler_params=pltpu.CompilerParams(
            collective_id=1, has_side_effects=True, vmem_limit_bytes=56 * 2**20
        ),
        cost_estimate=pl.CostEstimate(
            flops=4 * STEPS * slots * d * hs * 2, bytes_accessed=12 * 2**20, transcendentals=0
        ),
        name="layer",
    )(
        source_lengths, parents[:, 0], layer_in[:, 0], queries[:, 0], fresh_entries[:, 0],
        cross_queries[:, 0], jnp.transpose(past_cache[0], (1, 0, 2)), encoder_states[0],
        jnp.transpose(expert_ids[:, 0], (0, 2, 1)), jnp.transpose(gate_weights[:, 0], (0, 2, 1)),
        norm_gain, up_weight, down_weight,
    )
    layer_out, cache_out = pl.pallas_call(
        emit_kernel,
        out_shape=(
            jax.ShapeDtypeStruct((STEPS, SLOTS, d), BF16),
            jax.ShapeDtypeStruct((SLOTS * POS, 2 * d), BF16),
        ),
        in_specs=[vmem, vmem],
        out_specs=(hbm, hbm),
        scratch_shapes=[dma((2,))],
        name="emit",
    )(layer_out, cache_out)
    return layer_out[:, None], cache_out.reshape(1, SLOTS, POS, 2 * d)


def solution(mesh):
    in_specs = (
        P(None, "expert", "batch", None),
        P(None, "expert", "batch", None),
        P(None, "expert", "batch", None),
        P(None, "expert", "batch", None),
        P("expert", "batch", None, None),
        P("expert", "batch", None, None),
        P("expert", "batch"),
        P(None, "expert", None),
        P(None, "expert", None, None),
        P(None, "expert", None, None),
        P(),
        P("expert", None, "batch"),
        P("expert", "batch", None),
    )
    out_specs = (P(None, "expert", "batch", None), P("expert", "batch", None, None))
    return jax.shard_map(shards, mesh=mesh, in_specs=in_specs, out_specs=out_specs, check_vma=False)
```

time: 96.4 us -> 82.9 us (0.86)
  local copies, waits for them, and re-layouts: 10.5 us -> 0 us
  Pallas kernels: 84.9 us -> 82.2 us
    unnamed x5 -> x0, local copies, waits for them, and re-layouts: 9.25 us -> none
    pallas_call x1, Pallas kernels: 83.2 us -> 79.9 us  [shards(): pl.pallas_call(functools.partial(layer_kernel, ne), out_shape=(jax.ShapeD...]
    broadcast_in_dim x1 -> x0, local copies, waits for them, and re-layouts: 1.28 us -> none  [shards(): norm_gain[None]]
where the time goes in v2:
time: 82.9 us; the launch traced here: 82.8 us
  Pallas kernels  82.2 us (99%)
    pallas_call x1, Pallas kernels, shards(): pl.pallas_call(functools.partial(layer_kernel, ne), out_shape=(jax.ShapeD...  79.9 us
    pallas_call x1, Pallas kernels, shards(): pl.pallas_call(emit_kernel, out_shape=(jax.ShapeDtypeStruct((STEPS, SLOTS...  2.26 us

profile of v2, /device:TPU:1, one launch (start us, length us, event | category | flops | bytes accessed | tf_op | source)
XLA Modules:
  0.0 82.8 jit_solution(2594515138864622388)
XLA Ops:
  0.6 79.9 %layer.1 = (bf16[2,8,2048]{2,1,0:T(8,128)(2,1)}, bf16[128,4096]{1,0:T(8,128)(2,1)}) custom-call(s32[1,2]{1,0:T(1,128)} %lens.1, s32[2,64]{1,0:T(2,128)} %bitcast.29, bf16[2,8,2048]{2,1,0:T(8,128)(2,1)} %bitcast.23, bf16[2,8,2048]{2,1,0:T(8,128)(2,1)} %bitcast.24, bf16[2,8,4096]{2,1,0:T(8,128)(2,1)} %bitcast.22, bf16[2,8,2048]{2,1,0:T(8,128)(2,1)} %bitcast.25, ...), custom_call_target="tpu_custom_call" | custom-call | flops 4294967296 | bytes 12582912 | tf_op jit(solution)/shard_map/layer/pallas_call | solution.py:570
  80.6 2.3 %emit.1 = (bf16[2,8,2048]{2,1,0:T(8,128)(2,1)}, bf16[128,4096]{1,0:T(8,128)(2,1)}) custom-call(bf16[2,8,2048]{2,1,0:T(8,128)(2,1)} %get-tuple-element.6.layer_in, bf16[128,4096]{1,0:T(8,128)(2,1)} %get-tuple-element.7.cache_in), custom_call_target="tpu_custom_call" | custom-call | tf_op jit(solution)/shard_map/emit/pallas_call | solution.py:629

commit v3 on v2

--- a/solution.py
+++ b/solution.py
@@ -89,11 +89,11 @@
 
 def layer_kernel(
     ne,
-    lens, par, layer_in, queries, fresh, cross_q, cache, enc, ids, gates, gain, up_hbm, down_hbm,
+    lens, par, ids, gates, gain, cache_h, fresh_h, cross_h, enc_h, queries_h, layer_h, up_hbm, down_hbm,
     layer_out, cache_out,
-    wup, wdn, src0, src1, ext1, st_a, pool0, pool1, st_b, cross_s, resid,
+    cache, fresh, cross_q, enc, queries, layer_in, wup, wdn, src0, src1, ext1, st_a, pool0, pool1, st_b, cross_s, resid,
     pack_p, gate_hi, gate_lo, hsend, hrecv, psend, xb, hid, sib_s, sib_r, ysend, yrecv,
-    rsend, rrecv, fsend, frecv, wsem, lsem, csem, bsend, brecv, agsend, agrecv, sibsend, sibrecv,
+    rsend, rrecv, fsend, frecv, osem, wsem, lsem, csem, bsend, brecv, agsend, agrecv, sibsend, sibrecv,
 ):
     b, e = lax.axis_index("batch"), lax.axis_index("expert")
     y, c = b // 2, b % 2
@@ -103,6 +103,21 @@
     mc = d // NB
     slots = ne * PER
     unsent, unreceived = [], {}
+    operands = [
+        pltpu.make_async_copy(src, dst, osem.at[k])
+        for k, (src, dst) in enumerate(
+            (
+                (cache_h, cache),
+                (fresh_h, fresh),
+                (cross_h, cross_q),
+                (enc_h, enc),
+                (queries_h, queries),
+                (layer_h, layer_in),
+            )
+        )
+    ]
+    for copy in operands:
+        copy.start()
 
     def peer_y(q):
         return lax.rem(y + q, 4)
@@ -126,8 +141,6 @@
 
     up_copy = pltpu.make_async_copy(up_hbm, wup, wsem.at[0])
     down_copy = pltpu.make_async_copy(down_hbm, wdn, wsem.at[1])
-    up_copy.start()
-    down_copy.start()
 
     def local(src, dst):
         copy = pltpu.make_async_copy(src, dst, lsem)
@@ -137,8 +150,10 @@
     def wait_bytes(ref, sem):
         pltpu.make_async_copy(ref, ref, sem).wait()
 
-    def to_all(axis, t, phase, make, ref):
-        count = NB if axis == "batch" else ne
+    def to_all(t, phase, make, ref, axis="batch", span=(1, NB)):
+        if span[0] == span[1]:
+            unreceived[t, phase] = lambda: None
+            return
 
         def one(k, _):
             src, dst, to = make(k)
@@ -148,18 +163,25 @@
             ).start()
             return 0
 
-        lax.fori_loop(1, count, one, 0)
+        lax.fori_loop(span[0], span[1], one, 0)
         unsent.append(lambda: wait_bytes(ref, bsend.at[t, phase]))
         unreceived[t, phase] = lambda: wait_bytes(ref, brecv.at[t, phase])
 
+    mid = ne // 2
+    shift = 3 * ne // 4 if ne % 4 == 0 else 0
+    own_place = (ne - shift) % ne
+
+    def near_place(i):
+        return lax.rem(own_place + i, mid)
+
     def arrive(t, phase):
         unreceived.pop((t, phase))()
 
+    takes0, given0, given0_t, taken0, taken0_t = move_plan(par[0:1, :])
+
     near, late = CACHE * SLOTS, CACHE * SLOTS + 2 * POS
+    operands[0].wait()
     src0[0:near] = cache[...].astype(F32).reshape(near, 2 * d).astype(BF16)
-    blank = jnp.zeros((SLOTS, 2 * d), F32)
-    src0[late:] = jnp.concatenate([fresh[0].astype(F32), blank], axis=0).astype(BF16)
-    src1[late + POS :] = jnp.concatenate([fresh[1].astype(F32), blank], axis=0).astype(BF16)
 
     same_dev = iota((ROWS, ROWS), 0) // SLOTS == iota((ROWS, ROWS), 1) // SLOTS
     own_m = hot(iota((2 * POS, ROWS), 1) == 2 * b + iota((2 * POS, ROWS), 0) // POS)
@@ -170,7 +192,6 @@
         pick = dot(dot(own_m, chosen).astype(BF16), near_c)
         return dot(jnp.where(near_p, pick, 0.0).astype(BF16), src0[0:near])
 
-    takes0, given0, given0_t, taken0, taken0_t = move_plan(par[0:1, :])
     st_a[0] = given_rows(given0_t).astype(BF16)
 
     pl.semaphore_wait(barrier, NB - 1 + ne - 1)
@@ -188,7 +209,7 @@
             to = lax.rem(b + k, NB)
             return st_a.at[t, :, own_cols(to)], pools[t].at[own_rows(b)], to
 
-        to_all("batch", t, 0, make, st_b.at[t, pl.ds(0, 14 * POS)])
+        to_all(t, 0, make, st_b.at[t, pl.ds(0, 14 * POS)])
         local(st_a.at[t, :, own_cols(b)], pools[t].at[own_rows(b)])
 
     def send_b(t):
@@ -198,10 +219,16 @@
             to = lax.rem(b + k, NB)
             return st_b.at[t, own_rows(to)], landing.at[:, own_cols(b)], to
 
-        to_all("batch", t, 1, make, st_b.at[t, pl.ds(0, 14 * POS)])
+        to_all(t, 1, make, st_b.at[t, pl.ds(0, 14 * POS)])
         local(st_b.at[t, own_rows(b)], landing.at[:, own_cols(b)])
 
     send_a(0)
+    up_copy.start()
+    down_copy.start()
+    operands[1].wait()
+    blank = jnp.zeros((SLOTS, 2 * d), F32)
+    src0[late:] = jnp.concatenate([fresh[0].astype(F32), blank], axis=0).astype(BF16)
+    src1[late + POS :] = jnp.concatenate([fresh[1].astype(F32), blank], axis=0).astype(BF16)
 
     takes1, given1, given1_t, taken1, taken1_t = move_plan(par[1:2, :])
     kept1_t = dot(given1_t, jnp.where(same_dev, takes0.astype(F32), 0.0).astype(BF16)).astype(BF16)
@@ -216,15 +243,15 @@
     key_i = iota((SLOTS * HEADS, 64), 1)
     limit = jnp.where(own_s == 0, lens[0, 0], lens[0, 1])
     cross_valid = (key_i // 32 == own_s) & (key_i % 32 < limit)
-    enc_k = enc[:, :, :d].reshape(64, d)
-    enc_v = enc[:, :, d:].reshape(64, d)
 
     def cross(t):
+        enc_k = enc[:, :, :d].reshape(64, d)
+        enc_v = enc[:, :, d:].reshape(64, d)
         cross_s[t] = attend(cross_q[t].astype(F32), enc_k, enc_v, cross_valid)
 
     def route(t):
         slot = iota((slots, ROWS), 0)
-        owner = lax.rem(slot // PER + e, ne)
+        owner = lax.rem(slot // PER + shift + e, ne)
         expert = owner * 2 + slot % PER // CAP
         earlier = hot(iota((ROWS, ROWS), 0) < iota((ROWS, ROWS), 1))
         first = jnp.where(ids[t, 0:1, :] == expert, 1.0, 0.0)
@@ -279,6 +306,8 @@
     hand1_old = spread(dot(via1, from0))
     hand1_new = spread(dot(via1, given1))
     select0 = select(0, takes0, taken0)
+    for copy in operands[2:]:
+        copy.wait()
     cross(0)
 
     own_r = iota((SLOTS * HEADS, SLOTS * POS), 0) // HEADS
@@ -314,14 +343,15 @@
             to = lax.rem(b + k, NB)
             return hsend.at[t, to], hrecv.at[t, b], to
 
-        to_all("batch", t, 2, make, hsend.at[t, pl.ds(0, NB - 1)])
+        to_all(t, 2, make, hsend.at[t, pl.ds(0, NB - 1)])
         hrecv[t, b] = hsend[t, b]
 
     half = mc // 2
 
     def halves(x):
-        left = x[:, :half].reshape(ne, PER, half)
-        right = x[:, half:].reshape(ne, PER, half)
+        n = x.shape[0] // PER
+        left = x[:, :half].reshape(n, PER, half)
+        right = x[:, half:].reshape(n, PER, half)
         return jnp.concatenate([left, right], axis=1).astype(BF16)
 
     def whole(x):
@@ -335,11 +365,14 @@
         rows = hrecv[t].reshape(ROWS, mc).astype(BF16)
         psend[t] = halves(dot(pack_p[t], rows))
 
-        def make(k):
-            return psend.at[t, k], xb.at[t, b, k], lax.rem(e + k, ne)
-
-        to_all("expert", t, 3, make, psend.at[t, pl.ds(0, ne - 1)])
-        xb[t, b, 0] = psend[t, 0]
+        def make(s):
+            return psend.at[t, s], xb.at[t, b, s], lax.rem(e + s + shift, ne)
+
+        to_all(
+            t, 3, lambda i: make(near_place(i)), psend.at[t, pl.ds(0, mid - 1)], "expert", (1, mid)
+        )
+        to_all(t, 6, make, psend.at[t, pl.ds(0, mid)], "expert", (mid, ne))
+        xb[t, b, own_place] = psend[t, own_place]
 
     low, high = pl.ds(0, ne // 2), pl.ds(ne // 2, ne // 2)
     every = pl.ds(0, ne)
@@ -367,18 +400,23 @@
 
     def gather_start(t):
         arrive(t, 3)
-        for which in (1, 2, 3, 4, 0):
+        for which in (1, 4):
+            ag_copy(t, which).start()
+        arrive(t, 6)
+        for which in (2, 3, 0):
             ag_copy(t, which).start()
         for which in range(11):
             unsent.append(lambda which=which: ag_copy(t, which).wait_send())
 
-    def gather_relay(t):
-        for came, relay in ((1, 5), (2, 6)):
-            ag_copy(t, came).wait_recv()
-            ag_copy(t, relay).start()
-        for came, pass_on in ((3, 7), (4, 8)):
-            ag_copy(t, came).wait_recv()
-            ag_copy(t, pass_on).start()
+    def gather_relay(t, stage):
+        if stage == 0:
+            for came, relay in ((1, 5), (2, 6)):
+                ag_copy(t, came).wait_recv()
+                ag_copy(t, relay).start()
+        else:
+            for came, pass_on in ((3, 7), (4, 8)):
+                ag_copy(t, came).wait_recv()
+                ag_copy(t, pass_on).start()
 
     def up_part(t, block, first):
         x = whole(xb[t, block])
@@ -434,7 +472,7 @@
         ysend[t, which] = part.astype(BF16)
         y_copy(t, which).start()
 
-    def scatter_start(t):
+    def scatter_start(t, between):
         for q in range(4):
             unsent.append(lambda q=q: sib_copy(t, q).wait_send())
         for which in range(6):
@@ -451,6 +489,8 @@
         for q, after in ((2, 1), (1, 3), (3, 0), (0, None)):
             if after is not None:
                 for_sib(after)
+            if q == 3:
+                between()
             part = down_part(t, peer_y(q) * 2 + c, acts)
             sib_copy(t, q).wait_recv()
             part = part + sib_r[t, q]
@@ -473,20 +513,25 @@
         y_send(t, 5, sib_r[t, 3, second] + yrecv[t, 1].astype(F32))
 
     def give_back(t):
-        for which in range(2, 6):
+        def make(s):
+            return rsend.at[t, s], rrecv.at[t, s], lax.rem(e - s - shift + 2 * ne, ne)
+
+        for which in (2, 5):
             y_copy(t, which).wait_recv()
-        upper = sib_r[t, 0, first] + yrecv[t, 3].astype(F32) + yrecv[t, 4].astype(F32)
-        lower = sib_r[t, 0, second] + yrecv[t, 2].astype(F32) + yrecv[t, 5].astype(F32)
-        total = jnp.concatenate([upper, lower], axis=0)
-        rsend[t] = halves(total)
-
-        def make(k):
-            return rsend.at[t, k], rrecv.at[t, k], lax.rem(e - k + ne, ne)
-
-        to_all("expert", t, 4, make, rsend.at[t, pl.ds(0, ne - 1)])
-        rrecv[t, 0] = rsend[t, 0]
+        total = sib_r[t, 0, second] + yrecv[t, 2].astype(F32) + yrecv[t, 5].astype(F32)
+        rsend[t, mid:] = halves(total)
+        to_all(t, 7, make, rsend.at[t, pl.ds(0, mid)], "expert", (mid, ne))
+        for which in (3, 4):
+            y_copy(t, which).wait_recv()
+        total = sib_r[t, 0, first] + yrecv[t, 3].astype(F32) + yrecv[t, 4].astype(F32)
+        rsend[t, :mid] = halves(total)
+        to_all(
+            t, 4, lambda i: make(near_place(i)), rsend.at[t, pl.ds(0, mid - 1)], "expert", (1, mid)
+        )
+        rrecv[t, own_place] = rsend[t, own_place]
 
     def combine(t):
+        arrive(t, 7)
         arrive(t, 4)
         came = whole(rrecv[t])
         mixed = jnp.dot(gate_hi[t], came, preferred_element_type=F32) + jnp.dot(
@@ -498,7 +543,7 @@
             to = lax.rem(b + k, NB)
             return fsend.at[t, to], frecv.at[t, b], to
 
-        to_all("batch", t, 5, make, fsend.at[t, pl.ds(0, NB - 1)])
+        to_all(t, 5, make, fsend.at[t, pl.ds(0, NB - 1)])
         frecv[t, b] = fsend[t, b]
 
     def finish(t):
@@ -520,15 +565,16 @@
     gather_start(0)
     dispatch(1)
     up_copy.wait()
-    gather_relay(0)
+    gather_relay(0, 0)
+    gather_relay(0, 1)
     gather_start(1)
     gather_compute(0)
     down_copy.wait()
-    scatter_start(0)
-    gather_relay(1)
+    gather_relay(1, 0)
+    scatter_start(0, lambda: gather_relay(1, 1))
+    gather_compute(1)
     scatter_relay(0)
-    gather_compute(1)
-    scatter_start(1)
+    scatter_start(1, lambda: None)
     give_back(0)
     scatter_relay(1)
     give_back(1)
@@ -573,9 +619,15 @@
             jax.ShapeDtypeStruct((STEPS, SLOTS, d), BF16),
             jax.ShapeDtypeStruct((SLOTS * POS, 2 * d), BF16),
         ),
-        in_specs=[smem] + [vmem] * 10 + [hbm, hbm],
+        in_specs=[smem] + [vmem] * 4 + [hbm] * 8,
         out_specs=(vmem, hbm),
         scratch_shapes=[
+            pltpu.VMEM((CACHE, SLOTS, 2 * d), BF16),
+            pltpu.VMEM((STEPS, SLOTS, 2 * d), BF16),
+            pltpu.VMEM((STEPS, SLOTS, d), BF16),
+            pltpu.VMEM((2, 32, 2 * d), BF16),
+            pltpu.VMEM((STEPS, SLOTS, d), BF16),
+            pltpu.VMEM((STEPS, SLOTS, d), BF16),
             pltpu.VMEM((2, d, hs), BF16),
             pltpu.VMEM((2, hs, d), BF16),
             pltpu.VMEM((CACHE * SLOTS + 2 * POS + POS, 2 * d), BF16),
@@ -603,11 +655,12 @@
             pltpu.VMEM((STEPS, ne, 2 * PER, half), BF16),
             pltpu.VMEM((STEPS, NB, SLOTS, mc), F32),
             pltpu.VMEM((STEPS, NB, SLOTS, mc), F32),
+            dma((6,)),
             dma((2,)),
             dma,
             dma,
-            dma((STEPS, 6)),
-            dma((STEPS, 6)),
+            dma((STEPS, 8)),
+            dma((STEPS, 8)),
             dma((STEPS, 11)),
             dma((STEPS, 11)),
             dma((STEPS, 10)),
@@ -621,10 +674,10 @@
         ),
         name="layer",
     )(
-        source_lengths, parents[:, 0], layer_in[:, 0], queries[:, 0], fresh_entries[:, 0],
-        cross_queries[:, 0], jnp.transpose(past_cache[0], (1, 0, 2)), encoder_states[0],
-        jnp.transpose(expert_ids[:, 0], (0, 2, 1)), jnp.transpose(gate_weights[:, 0], (0, 2, 1)),
-        norm_gain, up_weight, down_weight,
+        source_lengths, parents[:, 0], jnp.transpose(expert_ids[:, 0], (0, 2, 1)),
+        jnp.transpose(gate_weights[:, 0], (0, 2, 1)), norm_gain,
+        jnp.transpose(past_cache[0], (1, 0, 2)), fresh_entries[:, 0], cross_queries[:, 0],
+        encoder_states[0], queries[:, 0], layer_in[:, 0], up_weight, down_weight,
     )
     layer_out, cache_out = pl.pallas_call(
         emit_kernel,

time: 82.9 us -> 80 us (0.965)
  Pallas kernels: 82.2 us -> 79.2 us
    pallas_call x1, Pallas kernels: 79.9 us -> 76.9 us  [shards(): pl.pallas_call(functools.partial(layer_kernel, ne), out_shape=(jax.ShapeD...]
where the time goes in v3:
time: 80 us; the launch traced here: 79.8 us
  Pallas kernels  79.2 us (99%)
    pallas_call x1, Pallas kernels, shards(): pl.pallas_call(functools.partial(layer_kernel, ne), out_shape=(jax.ShapeD...  76.9 us
    pallas_call x1, Pallas kernels, shards(): pl.pallas_call(emit_kernel, out_shape=(jax.ShapeDtypeStruct((STEPS, SLOTS...  2.26 us

profile of v3, /device:TPU:1, one launch (start us, length us, event | category | flops | bytes accessed | tf_op | source)
XLA Modules:
  0.0 79.8 jit_solution(7348834557473603539)
XLA Ops:
  0.6 76.9 %layer.1 = (bf16[2,8,2048]{2,1,0:T(8,128)(2,1)}, bf16[128,4096]{1,0:T(8,128)(2,1)}) custom-call(s32[1,2]{1,0:T(1,128)} %lens.1, s32[2,64]{1,0:T(2,128)} %bitcast.29, s32[2,2,64]{2,1,0:T(2,128)} %bitcast.27, f32[2,2,64]{2,1,0:T(2,128)} %bitcast.28, bf16[2048]{0:T(1024)(128)(2,1)} %gain.1, bf16[14,8,4096]{2,1,0:T(8,128)(2,1)} %bitcast.20, ...), custom_call_target="tpu_custom_call" | custom-call | flops 4294967296 | bytes 12582912 | tf_op jit(solution)/shard_map/layer/pallas_call | solution.py:616
  77.6 2.3 %emit.1 = (bf16[2,8,2048]{2,1,0:T(8,128)(2,1)}, bf16[128,4096]{1,0:T(8,128)(2,1)}) custom-call(bf16[2,8,2048]{2,1,0:T(8,128)(2,1)} %get-tuple-element.6.layer_in, bf16[128,4096]{1,0:T(8,128)(2,1)} %get-tuple-element.7.cache_in), custom_call_target="tpu_custom_call" | custom-call | tf_op jit(solution)/shard_map/emit/pallas_call | solution.py:682

commit v4 on v3

--- a/solution.py
+++ b/solution.py
@@ -142,10 +142,16 @@
     up_copy = pltpu.make_async_copy(up_hbm, wup, wsem.at[0])
     down_copy = pltpu.make_async_copy(down_hbm, wdn, wsem.at[1])
 
-    def local(src, dst):
-        copy = pltpu.make_async_copy(src, dst, lsem)
+    def local(t, phase, src, dst):
+        copy = pltpu.make_async_copy(src, dst, lsem.at[t, phase])
         copy.start()
-        copy.wait()
+        others = unreceived[t, phase]
+
+        def both():
+            others()
+            copy.wait()
+
+        unreceived[t, phase] = both
 
     def wait_bytes(ref, sem):
         pltpu.make_async_copy(ref, ref, sem).wait()
@@ -210,7 +216,7 @@
             return st_a.at[t, :, own_cols(to)], pools[t].at[own_rows(b)], to
 
         to_all(t, 0, make, st_b.at[t, pl.ds(0, 14 * POS)])
-        local(st_a.at[t, :, own_cols(b)], pools[t].at[own_rows(b)])
+        local(t, 0, st_a.at[t, :, own_cols(b)], pools[t].at[own_rows(b)])
 
     def send_b(t):
         landing = src0.at[near:late] if t == 0 else src1.at[SLOTS * POS : SLOTS * POS + 2 * POS]
@@ -220,7 +226,7 @@
             return st_b.at[t, own_rows(to)], landing.at[:, own_cols(b)], to
 
         to_all(t, 1, make, st_b.at[t, pl.ds(0, 14 * POS)])
-        local(st_b.at[t, own_rows(b)], landing.at[:, own_cols(b)])
+        local(t, 1, st_b.at[t, own_rows(b)], landing.at[:, own_cols(b)])
 
     send_a(0)
     up_copy.start()
@@ -238,6 +244,7 @@
     entry = dot(dot(own_m, given1_t).astype(BF16), slot_c)
     entry = jnp.where(iota((2 * POS, POS), 0) % POS == CACHE, entry, 0.0).astype(BF16)
     st_a[1] = (given_rows(kept1_t) + dot(entry, src0[late:])).astype(BF16)
+    send_a(1)
 
     own_s = iota((SLOTS * HEADS, 64), 0) // (HEADS * BEAM)
     key_i = iota((SLOTS * HEADS, 64), 1)
@@ -302,13 +309,15 @@
     arrive(0, 0)
     st_b[0] = dot(hand0, pool0[...]).astype(BF16)
     send_b(0)
-    send_a(1)
     hand1_old = spread(dot(via1, from0))
     hand1_new = spread(dot(via1, given1))
     select0 = select(0, takes0, taken0)
     for copy in operands[2:]:
         copy.wait()
     cross(0)
+    arrive(1, 0)
+    st_b[1] = (dot(hand1_old, pool0[...]) + dot(hand1_new, pool1[...])).astype(BF16)
+    send_b(1)
 
     own_r = iota((SLOTS * HEADS, SLOTS * POS), 0) // HEADS
     self_key = iota((SLOTS * HEADS, SLOTS * POS), 1)
@@ -428,7 +437,7 @@
             else:
                 hid[k] += part
 
-    def gather_compute(t):
+    def gather_compute(t, between):
         up_part(t, b, True)
         ag_copy(t, 0).wait_recv()
         up_part(t, sib, False)
@@ -437,6 +446,7 @@
         for came, pass_on in ((5, 9), (6, 10)):
             ag_copy(t, came).wait_recv()
             ag_copy(t, pass_on).start()
+        between()
         ag_copy(t, 7).wait_recv()
         up_part(t, down_y + 1 - c, False)
         ag_copy(t, 8).wait_recv()
@@ -553,27 +563,23 @@
             layer_out[t, :, cols] = (resid[t, :, cols] + frecv[t, j]).astype(BF16)
 
     attention(0)
-    arrive(1, 0)
-    st_b[1] = (dot(hand1_old, pool0[...]) + dot(hand1_new, pool1[...])).astype(BF16)
-    send_b(1)
+    cross(1)
+    select1 = select(1, takes1, taken1)
     route(0)
+    attention(1)
     dispatch(0)
-    select1 = select(1, takes1, taken1)
-    cross(1)
-    attention(1)
     route(1)
+    dispatch(1)
     gather_start(0)
-    dispatch(1)
     up_copy.wait()
     gather_relay(0, 0)
+    gather_start(1)
     gather_relay(0, 1)
-    gather_start(1)
-    gather_compute(0)
+    gather_compute(0, lambda: None)
     down_copy.wait()
     gather_relay(1, 0)
     scatter_start(0, lambda: gather_relay(1, 1))
-    gather_compute(1)
-    scatter_relay(0)
+    gather_compute(1, lambda: scatter_relay(0))
     scatter_start(1, lambda: None)
     give_back(0)
     scatter_relay(1)
@@ -581,20 +587,27 @@
     combine(0)
     finish(0)
     combine(1)
-    finish(1)
-
     for done in unsent:
         done()
-
-
-def emit_kernel(layer_in, cache_in, layer_out, cache_out, sem):
-    copies = [
-        pltpu.make_async_copy(cache_in, cache_out, sem.at[0]),
-        pltpu.make_async_copy(layer_in, layer_out, sem.at[1]),
-    ]
-    for copy in copies:
+    finish(1)
+
+
+def emit_kernel(layer_in, cache_in, layer_out, cache_out, layer_v, cache_v, came, left):
+    parts = 4
+    rows = cache_v.shape[0] // parts
+    into, out = [], []
+    for k in range(parts):
+        part = pl.ds(k * rows, rows)
+        into.append(pltpu.make_async_copy(cache_in.at[part], cache_v.at[part], came.at[k]))
+        out.append(pltpu.make_async_copy(cache_v.at[part], cache_out.at[part], left.at[k]))
+    into.append(pltpu.make_async_copy(layer_in, layer_v, came.at[parts]))
+    out.append(pltpu.make_async_copy(layer_v, layer_out, left.at[parts]))
+    for copy in into:
         copy.start()
-    for copy in copies:
+    for first, then in zip(into, out):
+        first.wait()
+        then.start()
+    for copy in out:
         copy.wait()
 
 
@@ -657,7 +670,7 @@
             pltpu.VMEM((STEPS, NB, SLOTS, mc), F32),
             dma((6,)),
             dma((2,)),
-            dma,
+            dma((STEPS, 2)),
             dma,
             dma((STEPS, 8)),
             dma((STEPS, 8)),
@@ -685,9 +698,14 @@
             jax.ShapeDtypeStruct((STEPS, SLOTS, d), BF16),
             jax.ShapeDtypeStruct((SLOTS * POS, 2 * d), BF16),
         ),
-        in_specs=[vmem, vmem],
+        in_specs=[hbm, hbm],
         out_specs=(hbm, hbm),
-        scratch_shapes=[dma((2,))],
+        scratch_shapes=[
+            pltpu.VMEM((STEPS, SLOTS, d), BF16),
+            pltpu.VMEM((SLOTS * POS, 2 * d), BF16),
+            dma((5,)),
+            dma((5,)),
+        ],
         name="emit",
     )(layer_out, cache_out)
     return layer_out[:, None], cache_out.reshape(1, SLOTS, POS, 2 * d)

time: 80 us -> 77.9 us (0.974)
  Pallas kernels: 79.2 us -> 77.1 us
    pallas_call x1, Pallas kernels: 76.9 us -> 75.1 us  [shards(): pl.pallas_call(functools.partial(layer_kernel, ne), out_shape=(jax.ShapeD...]
where the time goes in v4:
time: 77.9 us; the launch traced here: 77.7 us
  Pallas kernels  77.1 us (99%)
    pallas_call x1, Pallas kernels, shards(): pl.pallas_call(functools.partial(layer_kernel, ne), out_shape=(jax.ShapeD...  75.1 us
    pallas_call x1, Pallas kernels, shards(): pl.pallas_call(emit_kernel, out_shape=(jax.ShapeDtypeStruct((STEPS, SLOTS...  2.01 us

profile of v4, /device:TPU:1, one launch (start us, length us, event | category | flops | bytes accessed | tf_op | source)
XLA Modules:
  0.0 77.7 jit_solution(4156838816126407532)
XLA Ops:
  0.6 75.1 %layer.1 = (bf16[2,8,2048]{2,1,0:T(8,128)(2,1)}, bf16[128,4096]{1,0:T(8,128)(2,1)}) custom-call(s32[1,2]{1,0:T(1,128)} %lens.1, s32[2,64]{1,0:T(2,128)} %bitcast.29, s32[2,2,64]{2,1,0:T(2,128)} %bitcast.27, f32[2,2,64]{2,1,0:T(2,128)} %bitcast.28, bf16[2048]{0:T(1024)(128)(2,1)} %gain.1, bf16[14,8,4096]{2,1,0:T(8,128)(2,1)} %bitcast.20, ...), custom_call_target="tpu_custom_call" | custom-call | flops 4294967296 | bytes 12582912 | tf_op jit(solution)/shard_map/layer/pallas_call | solution.py:629
  75.7 2.0 %emit.1 = (bf16[2,8,2048]{2,1,0:T(8,128)(2,1)}, bf16[128,4096]{1,0:T(8,128)(2,1)}) custom-call(bf16[2,8,2048]{2,1,0:T(8,128)(2,1)} %get-tuple-element.6.layer_in, bf16[128,4096]{1,0:T(8,128)(2,1)} %get-tuple-element.7.cache_in), custom_call_target="tpu_custom_call" | custom-call | tf_op jit(solution)/shard_map/emit/pallas_call | solution.py:695

commit v5 on v4

--- a/solution.py
+++ b/solution.py
@@ -136,8 +136,8 @@
         )
         return 0
 
-    lax.fori_loop(1, NB, greet_b, 0)
-    lax.fori_loop(1, ne, greet_e, 0)
+    lax.fori_loop(1, NB, greet_b, 0, unroll=True)
+    lax.fori_loop(1, ne, greet_e, 0, unroll=True)
 
     up_copy = pltpu.make_async_copy(up_hbm, wup, wsem.at[0])
     down_copy = pltpu.make_async_copy(down_hbm, wdn, wsem.at[1])
@@ -169,7 +169,7 @@
             ).start()
             return 0
 
-        lax.fori_loop(span[0], span[1], one, 0)
+        lax.fori_loop(span[0], span[1], one, 0, unroll=True)
         unsent.append(lambda: wait_bytes(ref, bsend.at[t, phase]))
         unreceived[t, phase] = lambda: wait_bytes(ref, brecv.at[t, phase])
 

time: 77.9 us -> 77.5 us (level)
  no operation moved by 1% of the time
where the time goes in v5:
time: 77.5 us; the launch traced here: 77.4 us
  Pallas kernels  76.7 us (99%)
    pallas_call x1, Pallas kernels, shards(): pl.pallas_call(functools.partial(layer_kernel, ne), out_shape=(jax.ShapeD...  74.7 us
    pallas_call x1, Pallas kernels, shards(): pl.pallas_call(emit_kernel, out_shape=(jax.ShapeDtypeStruct((STEPS, SLOTS...  2.01 us

profile of v5, /device:TPU:1, one launch (start us, length us, event | category | flops | bytes accessed | tf_op | source)
XLA Modules:
  0.0 77.4 jit_solution(4254154359224216648)
XLA Ops:
  0.6 74.7 %layer.1 = (bf16[2,8,2048]{2,1,0:T(8,128)(2,1)}, bf16[128,4096]{1,0:T(8,128)(2,1)}) custom-call(s32[1,2]{1,0:T(1,128)} %lens.1, s32[2,64]{1,0:T(2,128)} %bitcast.29, s32[2,2,64]{2,1,0:T(2,128)} %bitcast.27, f32[2,2,64]{2,1,0:T(2,128)} %bitcast.28, bf16[2048]{0:T(1024)(128)(2,1)} %gain.1, bf16[14,8,4096]{2,1,0:T(8,128)(2,1)} %bitcast.20, ...), custom_call_target="tpu_custom_call" | custom-call | flops 4294967296 | bytes 12582912 | tf_op jit(solution)/shard_map/layer/pallas_call | solution.py:629
  75.4 2.0 %emit.1 = (bf16[2,8,2048]{2,1,0:T(8,128)(2,1)}, bf16[128,4096]{1,0:T(8,128)(2,1)}) custom-call(bf16[2,8,2048]{2,1,0:T(8,128)(2,1)} %get-tuple-element.6.layer_in, bf16[128,4096]{1,0:T(8,128)(2,1)} %get-tuple-element.7.cache_in), custom_call_target="tpu_custom_call" | custom-call | tf_op jit(solution)/shard_map/emit/pallas_call | solution.py:695
